TPU v7x, 32 devices: a whole 2x2x4 slice. The times are simulated.
32 devices in a mesh: wide: 16 (over z, x, core), narrow: 2 (over y).
Axes of the slice: x: 2, y: 2, z: 4, core: 2. Of those that a mesh axis runs over, the one named last changes fastest.
Arguments:
- resid: bfloat16 [1024, 5120], P('wide'), may hold values from -6 to 6
- final_gain: float32 [5120], replicated, may hold values from 0.25 to 1.75
- unembed: bfloat16 [16384, 5120], P('narrow', 'wide'), may hold values from -12 to 12
- labels: int32 [1024, 4], replicated, may hold values from 0 to 16383
- layer_in: bfloat16 [1024, 5120], P('wide'), may hold values from -6 to 6
- gate_value: bfloat16 [1024, 13824], P('wide', 'narrow'), may hold values from -0.29882812 to 2
- down_weight: bfloat16 [13824, 5120], P('narrow', 'wide'), may hold values from -0.078125 to 0.078125
- basis_in: bfloat16 [5120, 5120], P('wide', 'narrow'), may hold values from -0.078125 to 0.078125
- basis_out: bfloat16 [13824, 13824], P('narrow', 'wide'), may hold values from -0.0546875 to 0.0546875
Outputs:
- corrected: float32 [13824, 5120], P('wide', 'narrow')
All inputs are finite; a program needn't handle non-finite values.
Results may differ from a plain program's by a relative error of at most 0.002.
The roundings to bfloat16 on the way count: a program that leaves them out, or rounds other values in their place, can miss the bound.
Values may be sent and summed in bfloat16 or wider, within the bound.
No kernel may reach another device: no remote copies, remote signals or barrier semaphores. Data moves between devices by JAX's collectives and lax.ppermute only.
A program may use at most 192 MiB of HBM per device.

v0:
```python
import jax
import jax.numpy as jnp
from jax import lax
from jax.sharding import PartitionSpec as P

SEQ = 256
EXAMPLES = 4


EPSILON = 1e-05


def contract_last(left, right):
    return lax.dot_general(
        left, right, (((1,), (1,)), ((), ())), preferred_element_type=jnp.float32
    )


def per_device(
    resid, final_gain, unembed, labels, layer_in, gate_value, down_weight, basis_in, basis_out
):
    wide_count = lax.axis_size("wide")
    wide_place = lax.axis_index("wide")
    narrow_place = lax.axis_index("narrow")
    local_tokens, width = resid.shape
    all_tokens, samples = labels.shape
    column_part = width // wide_count
    vocab_part = unembed.shape[0]
    hidden_part = down_weight.shape[0]
    grad_rows = local_tokens * samples
    resid_cols, inputs_cols = (
        lax.all_to_all(resid, "wide", split_axis=1, concat_axis=0, tiled=True),
        lax.all_to_all(layer_in, "wide", split_axis=1, concat_axis=0, tiled=True),
    )
    resid_float = resid_cols.astype(jnp.float32)
    gain_cols = lax.dynamic_slice_in_dim(final_gain, wide_place * column_part, column_part, 0)
    square_sums = lax.psum(jnp.sum(resid_float * resid_float, axis=1), "wide")
    inverse = lax.rsqrt(square_sums / width + EPSILON)
    normed = (resid_float * inverse[:, None] * gain_cols).astype(jnp.bfloat16)
    logits = lax.psum_scatter(
        contract_last(normed, unembed), "wide", scatter_dimension=0, tiled=True
    )
    largest = lax.pmax(jnp.max(logits, axis=1), "narrow")
    scaled = jnp.exp(logits - largest[:, None])
    totals = lax.psum(jnp.sum(scaled, axis=1), "narrow")
    probs = (scaled / totals[:, None]).astype(jnp.bfloat16)
    common = jnp.dot(
        lax.all_gather(probs, "wide", axis=0, tiled=True),
        unembed,
        preferred_element_type=jnp.float32,
    )
    shifted = labels - narrow_place * vocab_part
    inside = ((shifted >= 0) & (shifted < vocab_part)).astype(jnp.float32)
    picked = (
        jnp.take(unembed, jnp.clip(shifted, 0, vocab_part - 1), axis=0).astype(jnp.float32)
        * inside[:, :, None]
    )
    label_part = (common[:, None, :] - picked).reshape(all_tokens * samples, column_part)
    label_grads = lax.psum(label_part, "narrow")
    grads_local = lax.all_to_all(
        label_grads, "wide", split_axis=0, concat_axis=1, tiled=True
    ).reshape(local_tokens, samples, width)
    resid_local = resid.astype(jnp.float32)
    inverse_local = lax.rsqrt(jnp.mean(resid_local * resid_local, axis=1) + EPSILON)
    inner = jnp.sum(final_gain * grads_local * resid_local[:, None, :], axis=2)
    back = (
        inverse_local[:, None, None] * final_gain * grads_local
        - resid_local[:, None, :] * (inverse_local**3)[:, None, None] * inner[:, :, None] / width
    )
    back = back.astype(jnp.bfloat16).reshape(grad_rows, width)
    hidden_grads = contract_last(back, lax.all_gather(down_weight, "wide", axis=1, tiled=True))
    gated = (
        hidden_grads.reshape(local_tokens, samples, hidden_part)
        * gate_value.astype(jnp.float32)[:, None, :]
    )
    gated = gated.astype(jnp.bfloat16).reshape(grad_rows, hidden_part)
    rotated_part = jnp.dot(
        lax.all_gather(gated, "wide", axis=0, tiled=True),
        basis_out,
        preferred_element_type=jnp.float32,
    )
    rotated = lax.psum(rotated_part, "narrow").astype(jnp.bfloat16)
    inputs_part = jnp.dot(inputs_cols, basis_in, preferred_element_type=jnp.float32)
    inputs_rot = lax.psum(inputs_part, "wide").astype(jnp.bfloat16)
    rot_blocks = rotated.reshape(EXAMPLES, SEQ, samples, rotated.shape[1])
    input_blocks = inputs_rot.reshape(EXAMPLES, SEQ, inputs_rot.shape[1])
    blocks = jnp.einsum(
        "etsj,etd->esjd", rot_blocks, input_blocks, preferred_element_type=jnp.float32
    )
    return jnp.mean(blocks * blocks, axis=(0, 1))


def solution(mesh):
    in_specs = (
        P("wide", None),
        P(),
        P("narrow", "wide"),
        P(),
        P("wide", None),
        P("wide", "narrow"),
        P("narrow", "wide"),
        P("wide", "narrow"),
        P("narrow", "wide"),
    )
    out_specs = P("wide", "narrow")
    return jax.shard_map(
        per_device, mesh=mesh, in_specs=in_specs, out_specs=out_specs, check_vma=False
    )
```

profile of v0, /device:TPU:0, one launch (start us, length us, event | category | flops | bytes accessed | tf_op | source)
XLA Modules:
  0.0 2176.3 jit_solution(8388513209508192469)
XLA Ops:
  6.5 1.9 all_to_all.36
  8.4 1.1 copy.25
  9.5 7.4 all-to-all-start
  16.9 1.8 all_to_all.41
  18.6 1.1 copy.36
  19.7 15.9 all-to-all-done
  35.6 5.5 all-to-all-start.2
  41.1 0.1 dynamic_slice.3
  41.2 0.2 multiply_reduce_fusion.2
  41.4 0.1 reduce_sum.52
  41.5 18.3 all-to-all-done.2
  59.8 5.5 fusion.16
  65.2 224.9 %all-reduce.6 = (bf16[1024,2560]{1,0:T(8,128)(2,1)}, f32[1024]{0:T(1024)S(1)}) all-reduce(f32[1024,2560]{1,0:T(8,128)} %fusion.16, f32[1024]{0:T(1024)S(1)} %reduce_sum.52), channel_id=1, replica_groups=mesh['wide'=16,'narrow'=2] {'wide'}, use_global_device_ids=true, to_apply=%region_11.12 | all-reduce | flops 2622464 | bytes 15736832 | tf_op jit(solution)/shard_map/psum | solution.py:84
  290.1 0.3 fusion.12
  290.4 16.9 fusion.13
  307.4 334.7 %reduce-scatter.2.cloned.1.call-done = f32[64,8192]{1,0:T(8,128)} async-done(((f32[1024,8192]{1,0:T(8,128)}), f32[64,8192]{1,0:T(8,128)}) %reduce-scatter.2.cloned.1.call-update) | async-done | bytes 2097168 | tf_op jit(solution)/shard_map/reduce_scatter | solution.py:40
  642.1 1.8 reduce_max.9
  643.9 4.9 pmax.7
  648.8 2.0 fusion.10
  650.9 4.9 psum.36
  655.8 3.0 divide_convert_fusion
  658.8 0.6 all-reduce.5.cloned.1.call-start
  659.4 8.2 copy.29
  667.7 0.2 copy.28
  667.9 0.3 reshape.116
  668.2 0.2 copy.30
  668.4 0.3 reshape.113
  668.7 0.3 copy.27
  669.0 0.3 broadcast_in_dim.14
  669.3 20.3 gather_fusion
  689.6 95.3 %all-gather.4.cloned.1.call-done = bf16[1024,8192]{1,0:T(8,128)(2,1)} async-done(((bf16[64,8192]{1,0:T(8,128)(2,1)}), bf16[1024,8192]{1,0:T(8,128)(2,1)}) %all-gather.4.cloned.1.call-update) | async-done | bytes 16777232 | tf_op jit(solution)/shard_map/all_gather | solution.py:48
  784.9 13.5 fusion.14
  798.4 3.8 sub.32
  802.2 7.7 sub.33
  809.9 8.4 multiply_subtract_fusion
  818.3 6.3 copy.31
  824.7 0.5 all-gather.6.cloned.1.call-update
  825.2 128.3 %all-reduce.5.cloned.1.call-done = f32[16,256,320]{1,2,0:T(8,128)} async-done(((f32[16,256,320]{1,2,0:T(8,128)}), f32[16,256,320]{1,2,0:T(8,128)}) %all-reduce.5.cloned.1.call-update) | async-done | bytes 5242896 | tf_op jit(solution)/shard_map/psum | solution.py:59
  953.5 5.7 all-to-all-start.1
  959.2 0.2 all-gather.8.cloned.1.call-start
  959.4 0.1 mul.150
  959.5 4.8 mul.153
  964.2 8.4 mul.154
  972.6 1.3 convert_element_type.53
  974.0 0.2 multiply_reduce_fusion.3
  974.2 0.2 broadcast_multiply_fusion.2
  974.4 1.3 broadcast_multiply_fusion.1
  975.6 157.3 %all-to-all-done.1 = f32[16,256,320]{1,2,0:T(8,128)} async-done(((f32[16,256,320]{1,2,0:T(8,128)}), f32[16,256,320]{1,2,0:T(8,128)}, u32[]{:S(2)}, u32[]{:S(2)}) %all-to-all-start.1) | async-done | bytes 5242912 | tf_op jit(solution)/shard_map/all_to_all | solution.py:60
  1133.0 6.4 copy.32
  1139.4 6.4 multiply_reduce_fusion.1
  1145.8 0.1 mul.156
  1145.9 7.9 reshape.108
  1153.7 6.6 subtract_convert_fusion
  1160.3 221.0 %all-gather.6.cloned.1.call-done = bf16[6912,5120]{0,1:T(8,128)(2,1)} async-done(((bf16[6912,320]{0,1:T(8,128)(2,1)}), bf16[6912,5120]{0,1:T(8,128)(2,1)}) %all-gather.6.cloned.1.call-update) | async-done | bytes 70778896 | tf_op jit(solution)/shard_map/all_gather | solution.py:71
  1381.4 31.1 %fusion.5 = bf16[64,4,6912]{2,0,1:T(8,128)(2,1)} fusion(bf16[6912,5120]{0,1:T(8,128)(2,1)} %all-gather.6.cloned.1.call-done, f32[64,6912]{1,0:T(8,128)} %convert_element_type.53, bf16[64,4,5120]{2,1,0:T(4,128)(2,1)} %subtract_convert_fusion), kind=kOutput, calls=%fused_computation.5 | convolution fusion | flops 18122932224 | bytes 78708736 | tf_op jit(solution)/shard_map/dot_general | solution.py:14
  1412.4 6.5 copy.34
  1418.9 6.6 reshape.109
  1425.6 303.1 %all-gather.8.cloned.1.call-done = bf16[4096,6912]{1,0:T(8,128)(2,1)} async-done(((bf16[256,6912]{1,0:T(8,128)(2,1)}), bf16[4096,6912]{1,0:T(8,128)(2,1)}) %all-gather.8.cloned.1.call-update) | async-done | bytes 56623120 | tf_op jit(solution)/shard_map/all_gather | solution.py:78
  1728.7 58.4 %fusion.15 = f32[4096,864]{0,1:T(8,128)} fusion(bf16[4096,6912]{1,0:T(8,128)(2,1)} %all-gather.8.cloned.1.call-done, bf16[6912,864]{0,1:T(8,128)(2,1)} %param.17), kind=kOutput, calls=%fused_computation.31 | convolution fusion | flops 48922361856 | bytes 82722816 | tf_op jit(solution)/shard_map/dot_general | solution.py:77
  1787.2 325.5 %all-reduce.7 = bf16[4096,864]{0,1:T(8,128)(2,1)} all-reduce(f32[4096,864]{0,1:T(8,128)} %fusion.15), channel_id=1, replica_groups=mesh['wide'=16,'narrow'=2] {'narrow'}, use_global_device_ids=true, to_apply=%region_10.11 | all-reduce | flops 3538944 | bytes 21233664 | tf_op jit(solution)/shard_map/psum | solution.py:82
  2112.7 11.0 copy.35
  2123.7 12.9 reshape.110
  2136.5 28.6 %multiply_reduce_fusion = f32[864,2560]{1,0:T(8,128)S(1)} fusion(bf16[4,256,2560,1]{2,1,3,0:T(8,128)(2,1)} %bitcast.40, bf16[4,256,4,864]{3,2,1,0:T(4,128)(2,1)} %reshape.110), kind=kOutput, calls=%fused_computation.1 | convolution fusion | flops 18187960320 | bytes 21168128 | tf_op jit(solution)/shard_map/etsj,etd->esjd/dot_general | solution.py:87
  2165.1 4.4 broadcast_multiply_fusion
  (25 shorter events, 0.3 us)
Async XLA Ops:
  6.5 53.2 %copy-start = (bf16[320,2560]{1,0:T(8,128)(2,1)S(1)}, bf16[320,2560]{1,0:T(8,128)(2,1)}, u32[]{:S(2)}) copy-start(bf16[320,2560]{1,0:T(8,128)(2,1)} %param.16) | copy-start | bytes 4915204
  6.5 34.6 %copy-start.5 = (f32[5120]{0:T(1024)S(1)}, f32[5120]{0:T(1024)}, u32[]{:S(2)}) copy-start(f32[5120]{0:T(1024)} %param.10) | copy-start | bytes 61444
  9.5 26.1 %all-to-all-start = ((bf16[64,16,320]{2,0,1:T(8,128)(2,1)}), bf16[64,16,320]{2,0,1:T(8,128)(2,1)S(1)}, u32[]{:S(2)}, u32[]{:S(2)}) async-start(bf16[64,16,320]{2,0,1:T(8,128)(2,1)} %copy.25), calls=%async_computation | async-start | bytes 1572864 | tf_op jit(solution)/shard_map/all_to_all | solution.py:32
  35.6 24.2 %all-to-all-start.2 = ((bf16[64,16,320]{2,0,1:T(8,128)(2,1)}), bf16[64,16,320]{2,0,1:T(8,128)(2,1)S(1)}, u32[]{:S(2)}, u32[]{:S(2)}) async-start(bf16[64,16,320]{2,0,1:T(8,128)(2,1)} %copy.36), calls=%async_computation.3 | async-start | bytes 1572864 | tf_op jit(solution)/shard_map/all_to_all | solution.py:33
  41.1 601.0 %reduce-scatter.2.cloned.1.call-start = ((), (), s32[]{:S(2)}) async-start(), calls=%async_computation.4 | async-start | bytes 35651584 | tf_op jit(solution)/shard_map/reduce_scatter | solution.py:40
  307.3 477.6 %all-gather.4.cloned.1.call-start = ((), (), s32[]{:S(2)}) async-start(), calls=%async_computation.5 | async-start | bytes 17825792 | tf_op jit(solution)/shard_map/all_gather | solution.py:48
  658.8 294.7 %all-reduce.5.cloned.1.call-start = ((), (), s32[]{:S(2)}) async-start(), calls=%async_computation.6 | async-start | bytes 10485760 | tf_op jit(solution)/shard_map/psum | solution.py:59
  659.4 8.3 copy-start.6
  824.6 556.7 %all-gather.6.cloned.1.call-start = ((), (), s32[]{:S(2)}) async-start(), calls=%async_computation.7 | async-start | bytes 75202560 | tf_op jit(solution)/shard_map/all_gather | solution.py:71
  825.2 134.3 %copy-start.2 = (bf16[64,5120]{1,0:T(8,128)(2,1)S(1)}, bf16[64,5120]{1,0:T(8,128)(2,1)}, u32[]{:S(2)}) copy-start(bf16[64,5120]{1,0:T(8,128)(2,1)} %param.9) | copy-start | bytes 1966084
  953.5 179.5 %all-to-all-start.1 = ((f32[16,256,320]{1,2,0:T(8,128)}), f32[16,256,320]{1,2,0:T(8,128)}, u32[]{:S(2)}, u32[]{:S(2)}) async-start(f32[16,256,320]{1,2,0:T(8,128)} %all-reduce.5.cloned.1.call-done), calls=%async_computation.2 | async-start | bytes 10485760 | tf_op jit(solution)/shard_map/all_to_all | solution.py:60
  959.2 769.6 %all-gather.8.cloned.1.call-start = ((), (), s32[]{:S(2)}) async-start(), calls=%async_computation.8 | async-start | bytes 60162048 | tf_op jit(solution)/shard_map/all_gather | solution.py:78
  964.2 8.4 copy-start.4
  1145.9 7.9 copy-start.3
  2136.5 33.0 %copy-start.1 = (bf16[320,2560]{1,0:T(8,128)(2,1)S(1)}, bf16[320,2560]{1,0:T(8,128)(2,1)}, u32[]{:S(2)}) copy-start(bf16[320,2560]{1,0:T(8,128)(2,1)} %param.16) | copy-start | bytes 4915204
Sparse Core Ops, SparseCore 0:
  307.5 334.5 reduce-scatter.1
  658.9 125.9 all-gather.3
  824.7 128.7 all-reduce.4
  955.0 426.2 all-gather.5
  1425.7 302.9 all-gather.7
where the time goes:
time: 2180 us
  waiting for transfers between devices  1270 us (58%)
  blocking collectives  560 us (26%)
  matrix products  154 us (7%)
  local copies, waits for them, and re-layouts  118 us (5%)
  other arithmetic  36.1 us (2%)
    reduce_scatter x1, waiting for transfers between devices, per_device(): lax.psum_scatter(contract_last(normed, unembed), 'wide', scatter_dimensio...  335 us
    psum x1, blocking collectives, per_device(): rotated = lax.psum(rotated_part, 'narrow').astype(jnp.bfloat16)  325 us
    all_gather x1, waiting for transfers between devices, per_device(): lax.all_gather(gated, 'wide', axis=0, tiled=True)  303 us
    psum x1, blocking collectives, per_device(): inputs_rot = lax.psum(inputs_part, 'wide').astype(jnp.bfloat16)  225 us
    all_gather x1, waiting for transfers between devices, per_device(): lax.all_gather(down_weight, 'wide', axis=1, tiled=True)  221 us
    all_to_all x1, waiting for transfers between devices, per_device(): lax.all_to_all(label_grads, 'wide', split_axis=0, concat_axis=1, tiled=True)  157 us
    psum x1, waiting for transfers between devices, per_device(): label_grads = lax.psum(label_part, 'narrow')  128 us
    all_gather x1, waiting for transfers between devices, per_device(): lax.all_gather(probs, 'wide', axis=0, tiled=True)  95.3 us
  transfers between devices with their start and end apart: 8, of which 8 were waited for; matrix products, arithmetic and copies ran while one was open for 3% of the time, Pallas kernels for 0%

commit v1 on v0

v1 whole, which is shorter than its diff:
```python
import jax
import jax.numpy as jnp
from jax import lax
from jax.experimental import pallas as pl
from jax.experimental.pallas import tpu as pltpu
from jax.sharding import PartitionSpec as P

SEQ = 256
EPSILON = 1e-05
BF = jnp.bfloat16
F32 = jnp.float32


def dot(left, right, dims):
    return lax.dot_general(left, right, (dims, ((), ())), preferred_element_type=F32)


def after(arrays, first):
    return lax.optimization_barrier((arrays, first))[0]


def shift_pairs(chips, by_line, by_side, by_core):
    lines = chips // 2
    pairs = []
    for line in range(lines):
        for side in range(2):
            for core in range(2):
                there = ((line + by_line) % lines * 2 + (side + by_side) % 2) * 2 + (core + by_core) % 2
                pairs.append(((line * 2 + side) * 2 + core, there))
    return pairs


def swap_core(array):
    wide = lax.axis_size("wide")
    return lax.ppermute(array, "wide", [(i, i ^ 1) for i in range(wide)])


def join_core(array, axis):
    got = swap_core(array)
    core = lax.axis_index("wide") % 2
    return jnp.concatenate(
        [jnp.where(core == 0, array, got), jnp.where(core == 0, got, array)], axis=axis
    )


def swap_narrow(parts):
    if lax.axis_size("narrow") != 2:
        return lax.all_to_all(parts, "narrow", split_axis=0, concat_axis=0, tiled=True)
    me = lax.axis_index("narrow")
    got = lax.ppermute(
        jnp.where(me == 0, parts[1], parts[0]), "narrow", [(0, 1), (1, 0)]
    )
    return jnp.stack([jnp.where(me == 0, parts[0], got), jnp.where(me == 0, got, parts[1])])


def sum_narrow(parts):
    if lax.axis_size("narrow") != 2:
        return lax.psum_scatter(parts, "narrow", scatter_dimension=0, tiled=True)[0]
    me = lax.axis_index("narrow")
    got = lax.ppermute(
        jnp.where(me == 0, parts[1], parts[0]), "narrow", [(0, 1), (1, 0)]
    )
    return jnp.where(me == 0, parts[0], parts[1]) + got


def join_narrow(array, axis):
    if lax.axis_size("narrow") != 2:
        return lax.all_gather(array, "narrow", axis=axis, tiled=True)
    me = lax.axis_index("narrow")
    got = lax.ppermute(array, "narrow", [(0, 1), (1, 0)])
    return jnp.concatenate(
        [jnp.where(me == 0, array, got), jnp.where(me == 0, got, array)], axis=axis
    )


def ring_chip(place, chips):
    lines = chips // 2
    return jnp.where(place < lines, 2 * place, 2 * (chips - 1 - place) + 1)


def ring_gather(block, odd):
    wide = lax.axis_size("wide")
    chips = wide // 2
    lines = chips // 2
    order = [2 * i if i < lines else 2 * (chips - 1 - i) + 1 for i in range(chips)]
    chip = lax.axis_index("wide") // 2
    place = jnp.where(chip % 2 == 0, chip // 2, chips - 1 - chip // 2)
    size = block.shape[0]
    out = jnp.zeros((chips * size,) + block.shape[1:], block.dtype)
    out = lax.dynamic_update_slice_in_dim(out, block, chip * size, 0)
    many = chips // 2
    for step, hops in ((1, chips - 1 - many if odd else many), (-1, many if odd else chips - 1 - many)):
        pairs = [
            (2 * order[i] + core, 2 * order[(i + step) % chips] + core)
            for i in range(chips)
            for core in range(2)
        ]
        held = block
        for hop in range(1, hops + 1):
            held = lax.ppermute(held, "wide", pairs)
            source = ring_chip((place - step * hop) % chips, chips)
            out = lax.dynamic_update_slice_in_dim(out, held, source * size, 0)
    return out


def chip_exchange(array, axis):
    wide = lax.axis_size("wide")
    chips = wide // 2
    chip = lax.axis_index("wide") // 2
    line, side = chip // 2, chip % 2
    size = array.shape[axis] // chips
    shape = list(array.shape)
    shape[axis] = size
    out = jnp.zeros([chips] + shape, array.dtype)
    for by_line in range(chips // 2):
        for by_side in range(2):
            to = (line + by_line) % (chips // 2) * 2 + (side + by_side) % 2
            piece = lax.dynamic_slice_in_dim(array, to * size, size, axis)
            if by_line or by_side:
                piece = lax.ppermute(piece, "wide", shift_pairs(chips, by_line, by_side, 0))
            source = (line - by_line) % (chips // 2) * 2 + (side - by_side) % 2
            out = lax.dynamic_update_slice_in_dim(out, piece[None], source, 0)
    return out


def merge_stats(mine, got):
    largest = jnp.maximum(mine[0], got[0])
    a, b = jnp.exp(mine[0] - largest), jnp.exp(got[0] - largest)
    sums = mine[1:3] * a + got[1:3] * b
    return jnp.concatenate([largest[None], sums, mine[3:] + got[3:]])


def share_stats(stats):
    for axis in ("wide", "narrow"):
        count = lax.axis_size(axis)
        bit = 1
        while bit < count:
            got = lax.ppermute(stats, axis, [(i, i ^ bit) for i in range(count)])
            stats = merge_stats(stats, got)
            bit *= 2
    return stats


def square_kernel(samples, rotated_ref, inputs_ref, total_ref, out_ref):
    seq = inputs_ref.shape[1]
    total = total_ref[...]
    for s in range(samples):
        block = dot(rotated_ref[:, s * seq : (s + 1) * seq], inputs_ref[...], ((1,), (1,)))
        total = total + block * block
    out_ref[...] = total


def add_squares(rotated, inputs, total, samples):
    rows, dirs = rotated.shape[0], inputs.shape[0]
    row_block = 432 if rows % 432 == 0 else rows
    dir_block = 512 if dirs % 512 == 0 else dirs
    spec = pl.BlockSpec((row_block, dir_block), lambda i, j: (i, j))
    return pl.pallas_call(
        lambda *refs: square_kernel(samples, *refs),
        out_shape=jax.ShapeDtypeStruct((rows, dirs), F32),
        grid=(rows // row_block, dirs // dir_block),
        in_specs=[
            pl.BlockSpec((row_block, rotated.shape[1]), lambda i, j: (i, 0)),
            pl.BlockSpec((dir_block, inputs.shape[1]), lambda i, j: (j, 0)),
            spec,
        ],
        out_specs=spec,
        input_output_aliases={2: 0},
        compiler_params=pltpu.CompilerParams(vmem_limit_bytes=32 * 1024 * 1024),
        cost_estimate=pl.CostEstimate(
            flops=2 * rows * dirs * rotated.shape[1],
            bytes_accessed=8 * rows * dirs + 2 * rotated.size + 2 * inputs.size,
            transcendentals=0,
        ),
    )(rotated, inputs, total)


def per_device(
    resid, final_gain, unembed, labels, layer_in, gate_value, down_weight, basis_in, basis_out
):
    wide = lax.axis_size("wide")
    narrow = lax.axis_size("narrow")
    chips = wide // 2
    place = lax.axis_index("wide")
    chip, core = place // 2, place % 2
    narrow_place = lax.axis_index("narrow")
    width = resid.shape[1]
    tokens, samples = labels.shape
    examples = tokens // SEQ
    vocab_part = unembed.shape[0]
    hidden_part = down_weight.shape[0]
    vocab_own = vocab_part // wide
    hidden_own = hidden_part // chips
    chip_cols = width // chips
    step = tokens // (wide * narrow)
    owners = chips // examples
    few = owners * step

    def regroup(array):
        rest = array.shape[1:]
        array = array.reshape((examples, owners, 2, narrow, step) + rest)
        return jnp.transpose(array, (2, 0, 3, 1, 4) + tuple(range(5, 5 + len(rest)))).reshape(
            (tokens,) + rest
        )

    resid_all = regroup(lax.all_gather(resid, "wide", axis=0, tiled=True))
    unembed_own = lax.all_to_all(unembed.T, "wide", split_axis=1, concat_axis=0, tiled=True)
    labels_all = regroup(labels)

    resid_float = resid_all.astype(F32)
    inverse = lax.rsqrt(jnp.mean(resid_float * resid_float, axis=1) + EPSILON)
    normed = (resid_float * inverse[:, None] * final_gain).astype(BF)
    logits = dot(unembed_own, normed, ((0,), (1,)))
    first_own = narrow_place * vocab_part + place * vocab_own
    entry = lax.broadcasted_iota(jnp.int32, logits.shape, 0) + first_own
    own_max = jnp.max(logits, axis=0)
    own_exp = jnp.exp(logits - own_max)
    stats = [own_max, jnp.sum(own_exp, axis=0), jnp.sum(own_exp * logits, axis=0)]
    for s in range(samples):
        stats.append(jnp.sum(jnp.where(entry == labels_all[:, s], logits, 0.0), axis=0))
    stats = share_stats(jnp.stack(stats))
    probs = (jnp.exp(logits - stats[0]) / stats[1]).astype(BF)
    inner = stats[2] / stats[1] - stats[3:]
    shrink = inner * (inverse * inverse / width)

    unembed_chip = join_core(unembed.T, 0)
    basis_chip = join_core(basis_out.T, 0)

    probs = probs.reshape(vocab_own, 2, tokens // 2)
    keep = jnp.where(core == 0, probs[:, 0], probs[:, 1])
    give = swap_core(jnp.where(core == 0, probs[:, 1], probs[:, 0]))
    probs = jnp.concatenate(
        [jnp.where(core == 0, keep, give), jnp.where(core == 0, give, keep)], axis=0
    )

    def own(array):
        array = array.reshape((2, examples, narrow, few) + array.shape[1:])
        array = lax.dynamic_index_in_dim(array, core, 0, keepdims=False)
        return lax.dynamic_index_in_dim(array, narrow_place, 1, keepdims=False)

    order = lax.dynamic_index_in_dim(
        labels_all.reshape(2, examples, narrow, few, samples), core, 0, keepdims=False
    )
    order = jnp.transpose(order, (1, 0, 3, 2)).reshape(-1)
    shifted = order - narrow_place * vocab_part
    inside = (shifted >= 0) & (shifted < vocab_part)
    picked = jnp.take(unembed_chip.T, jnp.clip(shifted, 0, vocab_part - 1), axis=0)
    picked = jnp.where(inside[:, None], picked, jnp.zeros_like(picked))
    picked = sum_narrow(picked.reshape(narrow, examples, samples * few, chip_cols))

    resid_cols = lax.dynamic_slice_in_dim(own(resid_all), chip * chip_cols, chip_cols, 2)
    inverse_own = own(inverse)
    shrink_own = own(shrink.T)
    gain_cols = lax.dynamic_slice_in_dim(final_gain, chip * chip_cols, chip_cols, 0)

    down_late = after(down_weight, logits)
    down_own = chip_exchange(down_late.T, 1)
    down_own = join_narrow(down_own, 2)
    down_own = join_core(down_own[:, None], 1).reshape(width, narrow * hidden_own)
    gate_late = after(gate_value, logits)
    gates = chip_exchange(gate_late.T, 0)
    gates = gates.reshape(examples, owners, hidden_own, narrow, step)
    gates = swap_narrow(jnp.transpose(gates, (3, 2, 0, 1, 4)))
    gates = gates.reshape(narrow * hidden_own, examples, 1, few)

    layer_late, basis_late = after((layer_in, basis_in), stats)
    layer_all = lax.all_gather(layer_late, "wide", axis=0, tiled=True)
    basis_own = lax.all_to_all(basis_late, "wide", split_axis=1, concat_axis=0, tiled=True)
    inputs_own = dot(basis_own, layer_all, ((0,), (1,))).astype(BF)
    dirs_own = inputs_own.shape[0]
    inputs_own = inputs_own.reshape(dirs_own, examples, owners, 2, narrow, step)
    inputs_own = jnp.transpose(inputs_own, (0, 1, 3, 4, 2, 5)).reshape(dirs_own, tokens)
    inputs_rot = lax.all_gather(inputs_own, "wide", axis=0, tiled=True)

    out_part = basis_out.shape[1]
    corrected = jnp.zeros((out_part, inputs_rot.shape[0]), F32)
    for e in range(examples):
        span = few * narrow
        probs_e = ring_gather(probs[:, e * span : (e + 1) * span], e % 2)
        common = dot(unembed_chip, probs_e, ((1,), (0,)))
        common = sum_narrow(jnp.transpose(common.reshape(chip_cols, narrow, few), (1, 0, 2)))
        grads = common[:, None] - jnp.transpose(
            picked[e].reshape(samples, few, chip_cols), (2, 0, 1)
        ).astype(F32)
        back = inverse_own[e] * gain_cols[:, None, None] * grads
        back = back - resid_cols[e].T.astype(F32)[:, None] * shrink_own[e].T
        back = back.astype(BF).reshape(chip_cols, samples * few)
        back = ring_gather(back, e % 2)
        hidden = dot(down_own, back, ((0,), (0,))).reshape(narrow * hidden_own, samples, few)
        gated = (hidden * gates[:, e].astype(F32)).astype(BF)
        gated = swap_narrow(gated.reshape(narrow, hidden_own, samples, few))
        gated = jnp.transpose(gated, (1, 2, 0, 3)).reshape(hidden_own, samples * span)
        gated = ring_gather(gated, e % 2)
        rotated = dot(basis_chip, gated, ((1,), (0,)))
        rotated = rotated.reshape(2 * out_part, narrow, samples * span // narrow)
        rotated = sum_narrow(jnp.transpose(rotated, (1, 0, 2))).astype(BF)
        rotated = rotated.reshape(2, out_part, samples * span // narrow)
        keep = jnp.where(core == 0, rotated[0], rotated[1])
        give = swap_core(jnp.where(core == 0, rotated[1], rotated[0]))
        rotated = jnp.stack(
            [jnp.where(core == 0, keep, give), jnp.where(core == 0, give, keep)], axis=1
        )
        rotated = join_narrow(rotated, 2).reshape(out_part, 2, samples, span)
        rotated = jnp.transpose(rotated, (0, 2, 1, 3)).reshape(out_part, samples * SEQ)
        corrected = add_squares(
            rotated, inputs_rot[:, e * SEQ : (e + 1) * SEQ], corrected, samples
        )
    return corrected / (examples * samples)


def solution(mesh):
    in_specs = (
        P("wide", None),
        P(),
        P("narrow", "wide"),
        P(),
        P("wide", None),
        P("wide", "narrow"),
        P("narrow", "wide"),
        P("wide", "narrow"),
        P("narrow", "wide"),
    )
    out_specs = P("wide", "narrow")
    return jax.shard_map(
        per_device, mesh=mesh, in_specs=in_specs, out_specs=out_specs, check_vma=False
    )
```

time: 2180 us -> 1730 us (0.79); the launches traced: 2180 us -> 1700 us
  waiting for transfers between devices: 1270 us -> 558 us
  blocking collectives: 560 us -> 0 us
  local copies, waits for them, and re-layouts: 118 us -> 557 us
  starting transfers between devices: 19.4 us -> 263 us
  other arithmetic: 36.1 us -> 137 us
  Pallas kernels: 0 us -> 33.3 us
    all_gather x3, waiting for transfers between devices: 619 us -> 25 us  [the longest x1 25 us: per_device(): resid_all = regroup(lax.all_gather(resid, 'wide', axis=0, tiled=True))]
    psum x3 -> x0, blocking collectives: 555 us -> none  [the longest x1 325 us: per_device(): rotated = lax.psum(rotated_part, 'narrow').astype(jnp.bfloat16)]
    ppermute x0 -> x130, waiting for transfers between devices: none -> 486 us  [the longest x84 346 us: ring_gather(): held = lax.ppermute(held, 'wide', pairs)]
    reduce_scatter x1 -> x0, waiting for transfers between devices: 335 us -> none  [per_device(): lax.psum_scatter(contract_last(normed, unembed), 'wide', scatter_dimensio...]
    dynamic_update_slice x0 -> x106, local copies, waits for them, and re-layouts: none -> 331 us  [the longest x82 280 us: ring_gather(): out = lax.dynamic_update_slice_in_dim(out, held, source * size, 0)]
    ppermute x0 -> x130, starting transfers between devices: none -> 238 us  [the longest x84 95.5 us: ring_gather(): held = lax.ppermute(held, 'wide', pairs)]
    all_to_all x3 -> x2, waiting for transfers between devices: 191 us -> 45.1 us  [the longest x1 43.3 us: per_device(): lax.all_to_all(basis_late, 'wide', split_axis=1, concat_axis=0, tiled=True)]
    psum x1 -> x0, waiting for transfers between devices: 128 us -> none  [per_device(): label_grads = lax.psum(label_part, 'narrow')]
  transfers between devices with their start and end apart: 8 -> 135, of which waited for: 8 -> 78; matrix products, arithmetic and copies ran while one was open for 3% -> 47% of each run, Pallas kernels for 0% -> 0%
where the time goes in v1:
time: 1730 us; the launch traced here: 1700 us
  waiting for transfers between devices  558 us (32%)
  local copies, waits for them, and re-layouts  557 us (32%)
  starting transfers between devices  263 us (15%)
  matrix products  138 us (8%)
  other arithmetic  137 us (8%)
  Pallas kernels  33.3 us (2%)
    ppermute x84, waiting for transfers between devices, ring_gather(): held = lax.ppermute(held, 'wide', pairs)  346 us
    dynamic_update_slice x82, local copies, waits for them, and re-layouts, ring_gather(): out = lax.dynamic_update_slice_in_dim(out, held, source * size, 0)  280 us
    dot_general x14, matrix products, dot(): lax.dot_general(left, right, (dims, ((), ())), preferred_element_type=F32)  138 us
    ppermute x84, starting transfers between devices, ring_gather(): held = lax.ppermute(held, 'wide', pairs)  95.5 us
    ppermute x14, starting transfers between devices, chip_exchange(): piece = lax.ppermute(piece, 'wide', shift_pairs(chips, by_line, by_side, 0))  85.7 us
    ppermute x14, waiting for transfers between devices, chip_exchange(): piece = lax.ppermute(piece, 'wide', shift_pairs(chips, by_line, by_side, 0))  59.6 us
    ppermute x28, local copies, waits for them, and re-layouts, ring_gather(): held = lax.ppermute(held, 'wide', pairs)  50.3 us
    ppermute x9, waiting for transfers between devices, sum_narrow(): lax.ppermute(jnp.where(me == 0, parts[1], parts[0]), 'narrow', [(0, 1), (...  43.6 us
  transfers between devices with their start and end apart: 135, of which 78 were waited for; matrix products, arithmetic and copies ran while one was open for 47% of the time, Pallas kernels for 0%

profile of v1, /device:TPU:0, one launch (start us, length us, event | category | flops | bytes accessed | tf_op | source)
XLA Modules:
  0.0 1702.3 jit_solution(15336949891114469441)
XLA Ops:
  35.9 43.3 %all-to-all-done.1 = bf16[320,16,160]{0,2,1:T(8,128)(2,1)S(1)} async-done(((bf16[320,16,160]{0,2,1:T(8,128)(2,1)}), bf16[320,16,160]{0,2,1:T(8,128)(2,1)S(1)}, u32[]{:S(2)}, u32[]{:S(2)}) %all-to-all-start.1) | async-done | bytes 1638432 | tf_op jit(solution)/shard_map/all_to_all | solution.py:268
  80.5 18.2 %all-to-all-start = ((bf16[320,16,512]{2,0,1:T(8,128)(2,1)}), bf16[320,16,512]{2,0,1:T(8,128)(2,1)}, u32[]{:S(2)}, u32[]{:S(2)}) async-start(bf16[320,16,512]{2,0,1:T(8,128)(2,1)} %copy.290), calls=%async_computation | async-start | bytes 10485760 | tf_op jit(solution)/shard_map/all_to_all | solution.py:207
  125.6 13.3 gather_fusion
  148.0 25.1 %collective-permute-done.25 = bf16[4,256,640]{2,1,0:T(8,128)(2,1)} collective-permute-done((bf16[4,256,640]{2,1,0:T(8,128)(2,1)}, bf16[4,256,640]{2,1,0:T(8,128)(2,1)}, u32[]{:S(2)}, u32[]{:S(2)}) %collective-permute-start.25) | collective-permute-done | bytes 1310752 | tf_op jit(solution)/shard_map/ppermute | solution.py:60
  175.8 25.0 %all-gather.4.cloned.1.call-done = bf16[1024,5120]{1,0:T(8,128)(2,1)} async-done(((bf16[64,5120]{1,0:T(8,128)(2,1)}), bf16[1024,5120]{1,0:T(8,128)(2,1)}) %all-gather.4.cloned.1.call-update) | async-done | bytes 10485776 | tf_op jit(solution)/shard_map/all_gather | solution.py:206
  200.8 9.3 copy.301
  216.3 10.9 fusion.2
  227.1 9.1 copy.288
  238.1 10.4 fusion.66
  252.8 13.2 collective-permute-start.1
  266.0 38.6 %collective-permute-start.2 = (bf16[320,864]{1,0:T(8,128)(2,1)}, bf16[320,864]{1,0:T(8,128)(2,1)}, u32[]{:S(2)}, u32[]{:S(2)}) collective-permute-start(bf16[320,864]{1,0:T(8,128)(2,1)} %get-tuple-element.60), channel_id=1, source_target_pairs={{0,8},{2,10},{4,12},{6,14},{8,16},{10,18},{12,20},{14,22},{16,24},... | collective-permute-start | bytes 1658888 | tf_op jit(solution)/shard_map/ppermute | solution.py:120
  321.5 36.0 %collective-permute-start.12 = (f32[7,1024]{1,0:T(8,128)S(1)}, f32[7,1024]{1,0:T(8,128)S(1)}, u32[]{:S(2)}, u32[]{:S(2)}) collective-permute-start(f32[7,1024]{1,0:T(8,128)S(1)} %pad_maximum_fusion.13), channel_id=1, source_target_pairs={{0,4},{2,6},{4,0},{6,2},{8,12},{10,14},{12,8},{14,10},{16,20},{18,... | collective-permute-start | bytes 86024 | tf_op jit(solution)/shard_map/ppermute | solution.py:138
  378.9 10.7 collective-permute-done.35
  389.5 14.0 collective-permute-done.36
  403.9 11.7 collective-permute-done.37
  437.8 28.0 %collective-permute-start.6 = (bf16[320,864]{1,0:T(8,128)(2,1)S(1)}, bf16[320,864]{1,0:T(8,128)(2,1)S(1)}, u32[]{:S(2)}, u32[]{:S(2)}) collective-permute-start(bf16[320,864]{1,0:T(8,128)(2,1)S(1)} %copy-done.49), channel_id=1, source_target_pairs={{0,24},{2,26},{4,28},{6,30},{8,0},{10,2},{12,4},{14,6},{16,8},{18,... | collective-permute-start | bytes 1658888 | tf_op jit(solution)/shard_map/ppermute | solution.py:120
  781.1 11.2 broadcast_select_fusion.3
  865.5 15.8 collective-permute-done.68
  884.5 15.8 collective-permute-done.94
  903.3 15.8 collective-permute-done.120
  922.4 15.8 collective-permute-done.43
  941.3 15.8 collective-permute-done.69
  960.3 15.8 collective-permute-done.95
  980.1 14.9 collective-permute-done.121
  997.1 16.9 collective-permute-done.44
  1017.2 15.8 collective-permute-done.70
  1033.2 18.7 %collective-permute-done.96 = bf16[864,512]{1,0:T(8,128)(2,1)} collective-permute-done((bf16[864,512]{1,0:T(8,128)(2,1)}, bf16[864,512]{1,0:T(8,128)(2,1)}, u32[]{:S(2)}, u32[]{:S(2)}) %collective-permute-start.96) | collective-permute-done | bytes 884768 | tf_op jit(solution)/shard_map/ppermute | solution.py:100
  1052.2 16.3 broadcast_select_fusion.1
  1088.9 8.9 dynamic_update_slice.392
  1101.3 8.9 dynamic_update_slice.416
  1113.5 8.8 dynamic_update_slice.440
  1123.9 9.8 dynamic_update_slice.369
  1135.3 9.9 dynamic_update_slice.393
  1146.7 9.9 dynamic_update_slice.417
  1157.2 9.9 dynamic_update_slice.441
  1175.3 9.8 dynamic_update_slice.370
  1186.7 9.9 dynamic_update_slice.394
  1198.1 9.9 dynamic_update_slice.418
  1209.5 9.9 dynamic_update_slice.442
  1229.8 10.2 dynamic_update_slice.371
  1242.6 10.2 dynamic_update_slice.395
  1255.1 10.3 dynamic_update_slice.419
  1265.4 9.8 dynamic_update_slice.372
  1275.2 9.9 dynamic_update_slice.420
  1293.9 8.8 dynamic_update_slice.421
  1304.3 9.8 dynamic_update_slice.374
  1315.7 9.9 dynamic_update_slice.422
  1327.1 9.9 dynamic_update_slice.443
  1345.3 9.2 dynamic_update_slice.375
  1354.5 18.0 %fusion.53 = f32[1728,512]{1,0:T(8,128)S(1)} fusion(bf16[6912,512]{0,1:T(8,128)(2,1)} %dynamic_update_slice.375, bf16[864,6912]{1,0:T(8,128)(2,1)} %get-tuple-element.40, bf16[864,6912]{1,0:T(8,128)(2,1)} %get-tuple-element.39), kind=kOutput, calls=%fused_computation.333 | convolution fusion | flops 12278366208 | bytes 34504704 | tf_op jit(solution)/shard_map/dot_general | solution.py:15
  1376.8 9.6 dynamic_update_slice.396
  1386.4 10.2 dynamic_update_slice.397
  1396.6 9.2 dynamic_update_slice.398
  1405.8 10.3 dynamic_update_slice.399
  1416.1 18.0 %fusion.52 = f32[1728,512]{1,0:T(8,128)S(1)} fusion(bf16[6912,512]{0,1:T(8,128)(2,1)} %dynamic_update_slice.399, bf16[864,6912]{1,0:T(8,128)(2,1)} %get-tuple-element.40, bf16[864,6912]{1,0:T(8,128)(2,1)} %get-tuple-element.39), kind=kOutput, calls=%fused_computation.332 | convolution fusion | flops 12278366208 | bytes 34504704 | tf_op jit(solution)/shard_map/dot_general | solution.py:15
  1440.6 9.6 dynamic_update_slice.423
  1450.2 18.2 %fusion.51 = f32[1728,512]{1,0:T(8,128)S(1)} fusion(bf16[6912,512]{0,1:T(8,128)(2,1)} %dynamic_update_slice.423, bf16[864,6912]{1,0:T(8,128)(2,1)} %get-tuple-element.40, bf16[864,6912]{1,0:T(8,128)(2,1)} %get-tuple-element.39), kind=kOutput, calls=%fused_computation.331 | convolution fusion | flops 12278366208 | bytes 34504704 | tf_op jit(solution)/shard_map/dot_general | solution.py:15
  1473.6 9.6 dynamic_update_slice.444
  1483.3 10.2 dynamic_update_slice.445
  1493.5 9.2 dynamic_update_slice.446
  1502.7 10.3 dynamic_update_slice.447
  1513.0 18.2 %fusion.50 = f32[1728,512]{1,0:T(8,128)S(1)} fusion(bf16[6912,512]{0,1:T(8,128)(2,1)} %dynamic_update_slice.447, bf16[864,6912]{1,0:T(8,128)(2,1)} %get-tuple-element.40, bf16[864,6912]{1,0:T(8,128)(2,1)} %get-tuple-element.39), kind=kOutput, calls=%fused_computation.330 | convolution fusion | flops 12278366208 | bytes 34504704 | tf_op jit(solution)/shard_map/dot_general | solution.py:15
  1540.0 18.5 %collective-permute-done.127 = f32[1728,256]{1,0:T(8,128)S(1)} collective-permute-done((f32[1728,256]{1,0:T(8,128)S(1)}, f32[1728,256]{1,0:T(8,128)S(1)}, u32[]{:S(2)}, u32[]{:S(2)}) %collective-permute-start.127) | collective-permute-done | bytes 1769504 | tf_op jit(solution)/shard_map/ppermute | solution.py:60
  1567.6 14.2 collective-permute-done.51
  (686 shorter events, 783.7 us)
Async XLA Ops:
  6.5 194.3 %all-gather.4.cloned.1.call-start = ((), (), s32[]{:S(2)}) async-start(), calls=%async_computation.2 | async-start | bytes 11141120 | tf_op jit(solution)/shard_map/all_gather | solution.py:206
  7.3 301.8 %all-gather.6.cloned.1.call-start = ((), (), s32[]{:S(2)}) async-start(), calls=%async_computation.3 | async-start | bytes 11141120 | tf_op jit(solution)/shard_map/all_gather | solution.py:267
  8.0 91.5 %collective-permute-start.10 = (bf16[320,8192]{1,0:T(8,128)(2,1)}, bf16[320,8192]{1,0:T(8,128)(2,1)}, u32[]{:S(2)}, u32[]{:S(2)}) collective-permute-start(bf16[320,8192]{1,0:T(8,128)(2,1)} %bitcast.520), channel_id=1, source_target_pairs={{0,2},{2,0},{4,6},{6,4},{8,10},{10,8},{12,14},{14,12},{16,18},{18,... | collective-permute-start | bytes 15728648 | tf_op jit(solution)/shard_map/ppermute | solution.py:35
  12.3 66.9 %all-to-all-start.1 = ((bf16[320,16,160]{0,2,1:T(8,128)(2,1)}), bf16[320,16,160]{0,2,1:T(8,128)(2,1)S(1)}, u32[]{:S(2)}, u32[]{:S(2)}) async-start(bf16[320,16,160]{0,2,1:T(8,128)(2,1)} %bitcast.120), calls=%async_computation.1 | async-start | bytes 3932160 | tf_op jit(solution)/shard_map/all_to_all | solution.py:268
  80.5 157.5 %all-to-all-start = ((bf16[320,16,512]{2,0,1:T(8,128)(2,1)}), bf16[320,16,512]{2,0,1:T(8,128)(2,1)}, u32[]{:S(2)}, u32[]{:S(2)}) async-start(bf16[320,16,512]{2,0,1:T(8,128)(2,1)} %copy.290), calls=%async_computation | async-start | bytes 10485760 | tf_op jit(solution)/shard_map/all_to_all | solution.py:207
  98.8 969.7 %all-gather.8.cloned.1.call-start = ((), (), s32[]{:S(2)}) async-start(), calls=%async_computation.4 | async-start | bytes 5570560 | tf_op jit(solution)/shard_map/all_gather | solution.py:273
  141.8 31.3 %collective-permute-start.25 = (bf16[4,256,640]{2,1,0:T(8,128)(2,1)}, bf16[4,256,640]{2,1,0:T(8,128)(2,1)}, u32[]{:S(2)}, u32[]{:S(2)}) collective-permute-start(bf16[4,256,640]{2,1,0:T(8,128)(2,1)} %bitcast.71), channel_id=1, source_target_pairs={{0,1},{1,0},{2,3},{3,2},{4,5},{5,4},{6,7},{7,6},{8,9},{9,8},{10,11... | collective-permute-start | bytes 3932168 | tf_op jit(solution)/shard_map/ppermute | solution.py:60
  252.8 184.9 %collective-permute-start.1 = (bf16[320,864]{1,0:T(8,128)(2,1)}, bf16[320,864]{1,0:T(8,128)(2,1)}, u32[]{:S(2)}, u32[]{:S(2)}) collective-permute-start(bf16[320,864]{1,0:T(8,128)(2,1)} %get-tuple-element.61), channel_id=1, source_target_pairs={{0,4},{2,6},{4,0},{6,2},{8,12},{10,14},{12,8},{14,10},{16,20},{18,... | collective-permute-start | bytes 1658888 | tf_op jit(solution)/shard_map/ppermute | solution.py:120
  266.0 201.8 %collective-permute-start.2 = (bf16[320,864]{1,0:T(8,128)(2,1)}, bf16[320,864]{1,0:T(8,128)(2,1)}, u32[]{:S(2)}, u32[]{:S(2)}) collective-permute-start(bf16[320,864]{1,0:T(8,128)(2,1)} %get-tuple-element.60), channel_id=1, source_target_pairs={{0,8},{2,10},{4,12},{6,14},{8,16},{10,18},{12,20},{14,22},{16,24},... | collective-permute-start | bytes 1658888 | tf_op jit(solution)/shard_map/ppermute | solution.py:120
  304.6 165.3 %collective-permute-start.3 = (bf16[320,864]{1,0:T(8,128)(2,1)}, bf16[320,864]{1,0:T(8,128)(2,1)}, u32[]{:S(2)}, u32[]{:S(2)}) collective-permute-start(bf16[320,864]{1,0:T(8,128)(2,1)} %get-tuple-element.59), channel_id=1, source_target_pairs={{0,12},{2,14},{4,8},{6,10},{8,20},{10,22},{12,16},{14,18},{16,28},... | collective-permute-start | bytes 1658888 | tf_op jit(solution)/shard_map/ppermute | solution.py:120
  305.1 166.9 %collective-permute-start.4 = (bf16[320,864]{1,0:T(8,128)(2,1)}, bf16[320,864]{1,0:T(8,128)(2,1)}, u32[]{:S(2)}, u32[]{:S(2)}) collective-permute-start(bf16[320,864]{1,0:T(8,128)(2,1)} %get-tuple-element.58), channel_id=1, source_target_pairs={{0,16},{2,18},{4,20},{6,22},{8,24},{10,26},{12,28},{14,30},{16,0},... | collective-permute-start | bytes 1658888 | tf_op jit(solution)/shard_map/ppermute | solution.py:120
  321.5 40.9 %collective-permute-start.12 = (f32[7,1024]{1,0:T(8,128)S(1)}, f32[7,1024]{1,0:T(8,128)S(1)}, u32[]{:S(2)}, u32[]{:S(2)}) collective-permute-start(f32[7,1024]{1,0:T(8,128)S(1)} %pad_maximum_fusion.13), channel_id=1, source_target_pairs={{0,4},{2,6},{4,0},{6,2},{8,12},{10,14},{12,8},{14,10},{16,20},{18,... | collective-permute-start | bytes 86024 | tf_op jit(solution)/shard_map/ppermute | solution.py:138
  435.4 38.5 %collective-permute-start.5 = (bf16[320,864]{1,0:T(8,128)(2,1)}, bf16[320,864]{1,0:T(8,128)(2,1)}, u32[]{:S(2)}, u32[]{:S(2)}) collective-permute-start(bf16[320,864]{1,0:T(8,128)(2,1)} %get-tuple-element.57), channel_id=1, source_target_pairs={{0,20},{2,22},{4,16},{6,18},{8,28},{10,30},{12,24},{14,26},{16,4},... | collective-permute-start | bytes 1658888 | tf_op jit(solution)/shard_map/ppermute | solution.py:120
  437.8 38.1 %collective-permute-start.6 = (bf16[320,864]{1,0:T(8,128)(2,1)S(1)}, bf16[320,864]{1,0:T(8,128)(2,1)S(1)}, u32[]{:S(2)}, u32[]{:S(2)}) collective-permute-start(bf16[320,864]{1,0:T(8,128)(2,1)S(1)} %copy-done.49), channel_id=1, source_target_pairs={{0,24},{2,26},{4,28},{6,30},{8,0},{10,2},{12,4},{14,6},{16,8},{18,... | collective-permute-start | bytes 1658888 | tf_op jit(solution)/shard_map/ppermute | solution.py:120
  482.0 118.8 %collective-permute-start.8 = (bf16[8,320,864]{2,1,0:T(8,128)(2,1)}, bf16[8,320,864]{2,1,0:T(8,128)(2,1)}, u32[]{:S(2)}, u32[]{:S(2)}) collective-permute-start(bf16[8,320,864]{2,1,0:T(8,128)(2,1)} %bitcast_dynamic-update-slice_fusion.1), channel_id=1, source_target_pairs={{0,1},{1,0},{2,3},{3,2},{4,5},{5,4},{6,7},{7,6},{8,9},{9,8},{10,11... | collective-permute-start | bytes 13271048 | tf_op jit(solution)/shard_map/ppermute | solution.py:70
  502.5 22.5 %collective-permute-start.18 = (bf16[1024,128]{0,1:T(8,128)(2,1)S(1)}, bf16[1024,128]{0,1:T(8,128)(2,1)S(1)}, u32[]{:S(2)}, u32[]{:S(2)}) collective-permute-start(bf16[1024,128]{0,1:T(8,128)(2,1)S(1)} %collective-permute-done.17), channel_id=1, source_target_pairs={{0,8},{2,10},{8,16},{10,18},{16,24},{18,26},{24,28},{26,30},{28,20... | collective-permute-start | bytes 786440 | tf_op jit(solution)/shard_map/ppermute | solution.py:100
  552.4 22.5 %collective-permute-start.106 = (bf16[1024,128]{0,1:T(8,128)(2,1)S(1)}, bf16[1024,128]{0,1:T(8,128)(2,1)S(1)}, u32[]{:S(2)}, u32[]{:S(2)}) collective-permute-start(bf16[1024,128]{0,1:T(8,128)(2,1)S(1)} %collective-permute-done.105), channel_id=1, source_target_pairs={{0,8},{2,10},{8,16},{10,18},{16,24},{18,26},{24,28},{26,30},{28,20... | collective-permute-start | bytes 786440 | tf_op jit(solution)/shard_map/ppermute | solution.py:100
  580.6 32.2 %collective-permute-start.110 = (bf16[1024,128]{0,1:T(8,128)(2,1)}, bf16[1024,128]{0,1:T(8,128)(2,1)}, u32[]{:S(2)}, u32[]{:S(2)}) collective-permute-start(bf16[1024,128]{0,1:T(8,128)(2,1)} %collective-permute-done.109), channel_id=1, source_target_pairs={{0,4},{2,6},{8,0},{10,2},{16,8},{18,10},{24,16},{26,18},{28,24},{3... | collective-permute-start | bytes 786440 | tf_op jit(solution)/shard_map/ppermute | solution.py:100
  580.6 32.2 %collective-permute-start.58 = (bf16[1024,128]{0,1:T(8,128)(2,1)}, bf16[1024,128]{0,1:T(8,128)(2,1)}, u32[]{:S(2)}, u32[]{:S(2)}) collective-permute-start(bf16[1024,128]{0,1:T(8,128)(2,1)} %collective-permute-done.57), channel_id=1, source_target_pairs={{0,4},{2,6},{8,0},{10,2},{16,8},{18,10},{24,16},{26,18},{28,24},{3... | collective-permute-start | bytes 786440 | tf_op jit(solution)/shard_map/ppermute | solution.py:100
  597.9 42.1 %collective-permute-start.24 = (f32[640,64]{0,1:T(8,128)}, f32[640,64]{0,1:T(8,128)}, u32[]{:S(2)}, u32[]{:S(2)}) collective-permute-start(f32[640,64]{0,1:T(8,128)} %select_bitcast_fusion.26), channel_id=1, source_target_pairs={{0,1},{1,0},{2,3},{3,2},{4,5},{5,4},{6,7},{7,6},{8,9},{9,8},{10,11... | collective-permute-start | bytes 491528 | tf_op jit(solution)/shard_map/ppermute | solution.py:60
  611.9 169.2 %collective-permute-start.9 = (bf16[8,1,320,1728]{3,2,0,1:T(8,128)(2,1)}, bf16[8,1,320,1728]{3,2,0,1:T(8,128)(2,1)}, u32[]{:S(2)}, u32[]{:S(2)}) collective-permute-start(bf16[8,1,320,1728]{3,2,0,1:T(8,128)(2,1)} %maximum_bitcast_fusion), channel_id=1, source_target_pairs={{0,2},{2,0},{4,6},{6,4},{8,10},{10,8},{12,14},{14,12},{16,18},{18,... | collective-permute-start | bytes 26542088 | tf_op jit(solution)/shard_map/ppermute | solution.py:35
  643.6 24.7 %collective-permute-start.29 = (bf16[640,256]{0,1:T(8,128)(2,1)S(1)}, bf16[640,256]{0,1:T(8,128)(2,1)S(1)}, u32[]{:S(2)}, u32[]{:S(2)}) collective-permute-start(bf16[640,256]{0,1:T(8,128)(2,1)S(1)} %bitcast.553), channel_id=1, source_target_pairs={{0,4},{2,6},{8,0},{10,2},{16,8},{18,10},{24,16},{26,18},{28,24},{3... | collective-permute-start | bytes 983048 | tf_op jit(solution)/shard_map/ppermute | solution.py:100
  740.9 107.6 %collective-permute-start = (bf16[864,6912]{1,0:T(8,128)(2,1)}, bf16[864,6912]{1,0:T(8,128)(2,1)}, u32[]{:S(2)}, u32[]{:S(2)}) collective-permute-start(bf16[864,6912]{1,0:T(8,128)(2,1)} %bitcast), channel_id=1, source_target_pairs={{0,2},{2,0},{4,6},{6,4},{8,10},{10,8},{12,14},{14,12},{16,18},{18,... | collective-permute-start | bytes 35831816 | tf_op jit(solution)/shard_map/ppermute | solution.py:35
  808.2 28.2 %collective-permute-start.41 = (bf16[864,4,64]{0,2,1:T(8,128)(2,1)S(1)}, bf16[864,4,64]{0,2,1:T(8,128)(2,1)}, u32[]{:S(2)}, u32[]{:S(2)}) collective-permute-start(bf16[864,4,64]{0,2,1:T(8,128)(2,1)S(1)} %broadcast_select_fusion.21), channel_id=1, source_target_pairs={{0,1},{1,0},{2,3},{3,2},{4,5},{5,4},{6,7},{7,6},{8,9},{9,8},{10,11... | collective-permute-start | bytes 1327112 | tf_op jit(solution)/shard_map/ppermute | solution.py:50
  816.5 24.4 %collective-permute-start.67 = (bf16[864,4,64]{0,2,1:T(8,128)(2,1)}, bf16[864,4,64]{0,2,1:T(8,128)(2,1)}, u32[]{:S(2)}, u32[]{:S(2)}) collective-permute-start(bf16[864,4,64]{0,2,1:T(8,128)(2,1)} %broadcast_select_fusion.20), channel_id=1, source_target_pairs={{0,1},{1,0},{2,3},{3,2},{4,5},{5,4},{6,7},{7,6},{8,9},{9,8},{10,11... | collective-permute-start | bytes 1327112 | tf_op jit(solution)/shard_map/ppermute | solution.py:50
  839.4 22.9 %collective-permute-start.42 = (bf16[864,512]{1,0:T(8,128)(2,1)}, bf16[864,512]{1,0:T(8,128)(2,1)}, u32[]{:S(2)}, u32[]{:S(2)}) collective-permute-start(bf16[864,512]{1,0:T(8,128)(2,1)} %copy.307), channel_id=1, source_target_pairs={{0,8},{2,10},{8,16},{10,18},{16,24},{18,26},{24,28},{26,30},{28,20... | collective-permute-start | bytes 2654216 | tf_op jit(solution)/shard_map/ppermute | solution.py:100
  840.9 22.9 %collective-permute-start.45 = (bf16[864,512]{1,0:T(8,128)(2,1)}, bf16[864,512]{1,0:T(8,128)(2,1)}, u32[]{:S(2)}, u32[]{:S(2)}) collective-permute-start(bf16[864,512]{1,0:T(8,128)(2,1)} %copy.307), channel_id=1, source_target_pairs={{0,4},{2,6},{8,0},{10,2},{16,8},{18,10},{24,16},{26,18},{28,24},{3... | collective-permute-start | bytes 2654216 | tf_op jit(solution)/shard_map/ppermute | solution.py:100
  844.2 37.1 %collective-permute-start.68 = (bf16[864,512]{1,0:T(8,128)(2,1)}, bf16[864,512]{1,0:T(8,128)(2,1)}, u32[]{:S(2)}, u32[]{:S(2)}) collective-permute-start(bf16[864,512]{1,0:T(8,128)(2,1)} %copy.326), channel_id=1, source_target_pairs={{0,8},{2,10},{8,16},{10,18},{16,24},{18,26},{24,28},{26,30},{28,20... | collective-permute-start | bytes 2654216 | tf_op jit(solution)/shard_map/ppermute | solution.py:100
  848.5 34.3 %collective-permute-start.72 = (bf16[864,512]{1,0:T(8,128)(2,1)}, bf16[864,512]{1,0:T(8,128)(2,1)}, u32[]{:S(2)}, u32[]{:S(2)}) collective-permute-start(bf16[864,512]{1,0:T(8,128)(2,1)} %copy.326), channel_id=1, source_target_pairs={{0,4},{2,6},{8,0},{10,2},{16,8},{18,10},{24,16},{26,18},{28,24},{3... | collective-permute-start | bytes 2654216 | tf_op jit(solution)/shard_map/ppermute | solution.py:100
  849.0 51.2 %collective-permute-start.94 = (bf16[864,512]{1,0:T(8,128)(2,1)}, bf16[864,512]{1,0:T(8,128)(2,1)}, u32[]{:S(2)}, u32[]{:S(2)}) collective-permute-start(bf16[864,512]{1,0:T(8,128)(2,1)} %copy.340), channel_id=1, source_target_pairs={{0,8},{2,10},{8,16},{10,18},{16,24},{18,26},{24,28},{26,30},{28,20... | collective-permute-start | bytes 2654216 | tf_op jit(solution)/shard_map/ppermute | solution.py:100
  862.3 39.3 %collective-permute-start.97 = (bf16[864,512]{1,0:T(8,128)(2,1)}, bf16[864,512]{1,0:T(8,128)(2,1)S(1)}, u32[]{:S(2)}, u32[]{:S(2)}) collective-permute-start(bf16[864,512]{1,0:T(8,128)(2,1)} %copy.340), channel_id=1, source_target_pairs={{0,4},{2,6},{8,0},{10,2},{16,8},{18,10},{24,16},{26,18},{28,24},{3... | collective-permute-start | bytes 2654216 | tf_op jit(solution)/shard_map/ppermute | solution.py:100
  863.8 55.3 %collective-permute-start.120 = (bf16[864,512]{1,0:T(8,128)(2,1)}, bf16[864,512]{1,0:T(8,128)(2,1)S(1)}, u32[]{:S(2)}, u32[]{:S(2)}) collective-permute-start(bf16[864,512]{1,0:T(8,128)(2,1)} %copy.354), channel_id=1, source_target_pairs={{0,8},{2,10},{8,16},{10,18},{16,24},{18,26},{24,28},{26,30},{28,20... | collective-permute-start | bytes 2654216 | tf_op jit(solution)/shard_map/ppermute | solution.py:100
  881.3 39.4 %collective-permute-start.124 = (bf16[864,512]{1,0:T(8,128)(2,1)}, bf16[864,512]{1,0:T(8,128)(2,1)}, u32[]{:S(2)}, u32[]{:S(2)}) collective-permute-start(bf16[864,512]{1,0:T(8,128)(2,1)} %copy.354), channel_id=1, source_target_pairs={{0,4},{2,6},{8,0},{10,2},{16,8},{18,10},{24,16},{26,18},{28,24},{3... | collective-permute-start | bytes 2654216 | tf_op jit(solution)/shard_map/ppermute | solution.py:100
  882.7 55.4 %collective-permute-start.43 = (bf16[864,512]{1,0:T(8,128)(2,1)}, bf16[864,512]{1,0:T(8,128)(2,1)}, u32[]{:S(2)}, u32[]{:S(2)}) collective-permute-start(bf16[864,512]{1,0:T(8,128)(2,1)} %collective-permute-done.42), channel_id=1, source_target_pairs={{0,8},{2,10},{8,16},{10,18},{16,24},{18,26},{24,28},{26,30},{28,20... | collective-permute-start | bytes 2654216 | tf_op jit(solution)/shard_map/ppermute | solution.py:100
  900.2 39.4 %collective-permute-start.46 = (bf16[864,512]{1,0:T(8,128)(2,1)}, bf16[864,512]{1,0:T(8,128)(2,1)}, u32[]{:S(2)}, u32[]{:S(2)}) collective-permute-start(bf16[864,512]{1,0:T(8,128)(2,1)} %collective-permute-done.45), channel_id=1, source_target_pairs={{0,4},{2,6},{8,0},{10,2},{16,8},{18,10},{24,16},{26,18},{28,24},{3... | collective-permute-start | bytes 2654216 | tf_op jit(solution)/shard_map/ppermute | solution.py:100
  901.6 55.5 %collective-permute-start.69 = (bf16[864,512]{1,0:T(8,128)(2,1)}, bf16[864,512]{1,0:T(8,128)(2,1)}, u32[]{:S(2)}, u32[]{:S(2)}) collective-permute-start(bf16[864,512]{1,0:T(8,128)(2,1)} %collective-permute-done.68), channel_id=1, source_target_pairs={{0,8},{2,10},{8,16},{10,18},{16,24},{18,26},{24,28},{26,30},{28,20... | collective-permute-start | bytes 2654216 | tf_op jit(solution)/shard_map/ppermute | solution.py:100
  919.1 39.5 %collective-permute-start.73 = (bf16[864,512]{1,0:T(8,128)(2,1)}, bf16[864,512]{1,0:T(8,128)(2,1)}, u32[]{:S(2)}, u32[]{:S(2)}) collective-permute-start(bf16[864,512]{1,0:T(8,128)(2,1)} %collective-permute-done.72), channel_id=1, source_target_pairs={{0,4},{2,6},{8,0},{10,2},{16,8},{18,10},{24,16},{26,18},{28,24},{3... | collective-permute-start | bytes 2654216 | tf_op jit(solution)/shard_map/ppermute | solution.py:100
  920.6 55.4 %collective-permute-start.95 = (bf16[864,512]{1,0:T(8,128)(2,1)}, bf16[864,512]{1,0:T(8,128)(2,1)}, u32[]{:S(2)}, u32[]{:S(2)}) collective-permute-start(bf16[864,512]{1,0:T(8,128)(2,1)} %collective-permute-done.94), channel_id=1, source_target_pairs={{0,8},{2,10},{8,16},{10,18},{16,24},{18,26},{24,28},{26,30},{28,20... | collective-permute-start | bytes 2654216 | tf_op jit(solution)/shard_map/ppermute | solution.py:100
  938.2 39.3 %collective-permute-start.98 = (bf16[864,512]{1,0:T(8,128)(2,1)S(1)}, bf16[864,512]{1,0:T(8,128)(2,1)S(1)}, u32[]{:S(2)}, u32[]{:S(2)}) collective-permute-start(bf16[864,512]{1,0:T(8,128)(2,1)S(1)} %collective-permute-done.97), channel_id=1, source_target_pairs={{0,4},{2,6},{8,0},{10,2},{16,8},{18,10},{24,16},{26,18},{28,24},{3... | collective-permute-start | bytes 2654216 | tf_op jit(solution)/shard_map/ppermute | solution.py:100
  939.6 55.4 %collective-permute-start.121 = (bf16[864,512]{1,0:T(8,128)(2,1)S(1)}, bf16[864,512]{1,0:T(8,128)(2,1)}, u32[]{:S(2)}, u32[]{:S(2)}) collective-permute-start(bf16[864,512]{1,0:T(8,128)(2,1)S(1)} %collective-permute-done.120), channel_id=1, source_target_pairs={{0,8},{2,10},{8,16},{10,18},{16,24},{18,26},{24,28},{26,30},{28,20... | collective-permute-start | bytes 2654216 | tf_op jit(solution)/shard_map/ppermute | solution.py:100
  957.1 39.4 %collective-permute-start.125 = (bf16[864,512]{1,0:T(8,128)(2,1)}, bf16[864,512]{1,0:T(8,128)(2,1)}, u32[]{:S(2)}, u32[]{:S(2)}) collective-permute-start(bf16[864,512]{1,0:T(8,128)(2,1)} %collective-permute-done.124), channel_id=1, source_target_pairs={{0,4},{2,6},{8,0},{10,2},{16,8},{18,10},{24,16},{26,18},{28,24},{3... | collective-permute-start | bytes 2654216 | tf_op jit(solution)/shard_map/ppermute | solution.py:100
  958.6 55.4 %collective-permute-start.44 = (bf16[864,512]{1,0:T(8,128)(2,1)}, bf16[864,512]{1,0:T(8,128)(2,1)}, u32[]{:S(2)}, u32[]{:S(2)}) collective-permute-start(bf16[864,512]{1,0:T(8,128)(2,1)} %collective-permute-done.43), channel_id=1, source_target_pairs={{0,8},{2,10},{8,16},{10,18},{16,24},{18,26},{24,28},{26,30},{28,20... | collective-permute-start | bytes 2654216 | tf_op jit(solution)/shard_map/ppermute | solution.py:100
  976.1 39.4 %collective-permute-start.47 = (bf16[864,512]{1,0:T(8,128)(2,1)}, bf16[864,512]{1,0:T(8,128)(2,1)}, u32[]{:S(2)}, u32[]{:S(2)}) collective-permute-start(bf16[864,512]{1,0:T(8,128)(2,1)} %collective-permute-done.46), channel_id=1, source_target_pairs={{0,4},{2,6},{8,0},{10,2},{16,8},{18,10},{24,16},{26,18},{28,24},{3... | collective-permute-start | bytes 2654216 | tf_op jit(solution)/shard_map/ppermute | solution.py:100
  978.4 54.6 %collective-permute-start.70 = (bf16[864,512]{1,0:T(8,128)(2,1)}, bf16[864,512]{1,0:T(8,128)(2,1)}, u32[]{:S(2)}, u32[]{:S(2)}) collective-permute-start(bf16[864,512]{1,0:T(8,128)(2,1)} %collective-permute-done.69), channel_id=1, source_target_pairs={{0,8},{2,10},{8,16},{10,18},{16,24},{18,26},{24,28},{26,30},{28,20... | collective-permute-start | bytes 2654216 | tf_op jit(solution)/shard_map/ppermute | solution.py:100
  995.0 56.9 %collective-permute-start.96 = (bf16[864,512]{1,0:T(8,128)(2,1)}, bf16[864,512]{1,0:T(8,128)(2,1)}, u32[]{:S(2)}, u32[]{:S(2)}) collective-permute-start(bf16[864,512]{1,0:T(8,128)(2,1)} %collective-permute-done.95), channel_id=1, source_target_pairs={{0,8},{2,10},{8,16},{10,18},{16,24},{18,26},{24,28},{26,30},{28,20... | collective-permute-start | bytes 2654216 | tf_op jit(solution)/shard_map/ppermute | solution.py:100
  996.5 342.5 %collective-permute-start.74 = (bf16[864,512]{1,0:T(8,128)(2,1)}, bf16[864,512]{1,0:T(8,128)(2,1)}, u32[]{:S(2)}, u32[]{:S(2)}) collective-permute-start(bf16[864,512]{1,0:T(8,128)(2,1)} %collective-permute-done.73), channel_id=1, source_target_pairs={{0,4},{2,6},{8,0},{10,2},{16,8},{18,10},{24,16},{26,18},{28,24},{3... | collective-permute-start | bytes 2654216 | tf_op jit(solution)/shard_map/ppermute | solution.py:100
  1014.0 300.1 %collective-permute-start.99 = (bf16[864,512]{1,0:T(8,128)(2,1)}, bf16[864,512]{1,0:T(8,128)(2,1)}, u32[]{:S(2)}, u32[]{:S(2)}) collective-permute-start(bf16[864,512]{1,0:T(8,128)(2,1)} %copy-done.40), channel_id=1, source_target_pairs={{0,4},{2,6},{8,0},{10,2},{16,8},{18,10},{24,16},{26,18},{28,24},{3... | collective-permute-start | bytes 2654216 | tf_op jit(solution)/shard_map/ppermute | solution.py:100
  1015.4 310.1 %collective-permute-start.122 = (bf16[864,512]{1,0:T(8,128)(2,1)}, bf16[864,512]{1,0:T(8,128)(2,1)}, u32[]{:S(2)}, u32[]{:S(2)}) collective-permute-start(bf16[864,512]{1,0:T(8,128)(2,1)} %collective-permute-done.121), channel_id=1, source_target_pairs={{0,8},{2,10},{8,16},{10,18},{16,24},{18,26},{24,28},{26,30},{28,20... | collective-permute-start | bytes 2654216 | tf_op jit(solution)/shard_map/ppermute | solution.py:100
  1033.0 308.6 %collective-permute-start.126 = (bf16[864,512]{1,0:T(8,128)(2,1)}, bf16[864,512]{1,0:T(8,128)(2,1)}, u32[]{:S(2)}, u32[]{:S(2)}) collective-permute-start(bf16[864,512]{1,0:T(8,128)(2,1)} %collective-permute-done.125), channel_id=1, source_target_pairs={{0,4},{2,6},{8,0},{10,2},{16,8},{18,10},{24,16},{26,18},{28,24},{3... | collective-permute-start | bytes 2654216 | tf_op jit(solution)/shard_map/ppermute | solution.py:100
  1051.9 291.8 %collective-permute-start.48 = (bf16[864,512]{1,0:T(8,128)(2,1)}, bf16[864,512]{1,0:T(8,128)(2,1)}, u32[]{:S(2)}, u32[]{:S(2)}) collective-permute-start(bf16[864,512]{1,0:T(8,128)(2,1)} %collective-permute-done.47), channel_id=1, source_target_pairs={{0,4},{2,6},{8,0},{10,2},{16,8},{18,10},{24,16},{26,18},{28,24},{3... | collective-permute-start | bytes 2654216 | tf_op jit(solution)/shard_map/ppermute | solution.py:100
  1337.0 37.6 %collective-permute-start.71 = (bf16[864,512]{1,0:T(8,128)(2,1)}, bf16[864,512]{1,0:T(8,128)(2,1)}, u32[]{:S(2)}, u32[]{:S(2)}) collective-permute-start(bf16[864,512]{1,0:T(8,128)(2,1)} %collective-permute-done.70), channel_id=1, source_target_pairs={{0,8},{2,10},{8,16},{10,18},{16,24},{18,26},{24,28},{26,30},{28,20... | collective-permute-start | bytes 2654216 | tf_op jit(solution)/shard_map/ppermute | solution.py:100
  1337.3 101.1 %collective-permute-start.100 = (bf16[864,512]{1,0:T(8,128)(2,1)}, bf16[864,512]{1,0:T(8,128)(2,1)}, u32[]{:S(2)}, u32[]{:S(2)}) collective-permute-start(bf16[864,512]{1,0:T(8,128)(2,1)} %collective-permute-done.99), channel_id=1, source_target_pairs={{0,4},{2,6},{8,0},{10,2},{16,8},{18,10},{24,16},{26,18},{28,24},{3... | collective-permute-start | bytes 2654216 | tf_op jit(solution)/shard_map/ppermute | solution.py:100
  1339.0 132.4 %collective-permute-start.123 = (bf16[864,512]{1,0:T(8,128)(2,1)}, bf16[864,512]{1,0:T(8,128)(2,1)}, u32[]{:S(2)}, u32[]{:S(2)}) collective-permute-start(bf16[864,512]{1,0:T(8,128)(2,1)} %collective-permute-done.122), channel_id=1, source_target_pairs={{0,8},{2,10},{8,16},{10,18},{16,24},{18,26},{24,28},{26,30},{28,20... | collective-permute-start | bytes 2654216 | tf_op jit(solution)/shard_map/ppermute | solution.py:100
  1374.1 159.3 %collective-permute-start.49 = (f32[1728,256]{1,0:T(8,128)}, f32[1728,256]{1,0:T(8,128)}, u32[]{:S(2)}, u32[]{:S(2)}) collective-permute-start(f32[1728,256]{1,0:T(8,128)} %select_bitcast_fusion.3), channel_id=1, source_target_pairs={{0,1},{1,0},{2,3},{3,2},{4,5},{5,4},{6,7},{7,6},{8,9},{9,8},{10,11... | collective-permute-start | bytes 5308424 | tf_op jit(solution)/shard_map/ppermute | solution.py:60
  1436.7 98.6 %collective-permute-start.75 = (f32[1728,256]{1,0:T(8,128)}, f32[1728,256]{1,0:T(8,128)}, u32[]{:S(2)}, u32[]{:S(2)}) collective-permute-start(f32[1728,256]{1,0:T(8,128)} %select_bitcast_fusion.2), channel_id=1, source_target_pairs={{0,1},{1,0},{2,3},{3,2},{4,5},{5,4},{6,7},{7,6},{8,9},{9,8},{10,11... | collective-permute-start | bytes 5308424 | tf_op jit(solution)/shard_map/ppermute | solution.py:60
  1471.0 66.8 %collective-permute-start.101 = (f32[1728,256]{1,0:T(8,128)}, f32[1728,256]{1,0:T(8,128)}, u32[]{:S(2)}, u32[]{:S(2)}) collective-permute-start(f32[1728,256]{1,0:T(8,128)} %select_bitcast_fusion.1), channel_id=1, source_target_pairs={{0,1},{1,0},{2,3},{3,2},{4,5},{5,4},{6,7},{7,6},{8,9},{9,8},{10,11... | collective-permute-start | bytes 5308424 | tf_op jit(solution)/shard_map/ppermute | solution.py:60
  1531.7 26.8 %collective-permute-start.127 = (f32[1728,256]{1,0:T(8,128)S(1)}, f32[1728,256]{1,0:T(8,128)S(1)}, u32[]{:S(2)}, u32[]{:S(2)}) collective-permute-start(f32[1728,256]{1,0:T(8,128)S(1)} %select_bitcast_fusion), channel_id=1, source_target_pairs={{0,1},{1,0},{2,3},{3,2},{4,5},{5,4},{6,7},{7,6},{8,9},{9,8},{10,11... | collective-permute-start | bytes 5308424 | tf_op jit(solution)/shard_map/ppermute | solution.py:60
  1535.3 23.8 %collective-permute-start.50 = (bf16[864,256]{1,0:T(8,128)(2,1)S(1)}, bf16[864,256]{1,0:T(8,128)(2,1)S(1)}, u32[]{:S(2)}, u32[]{:S(2)}) collective-permute-start(bf16[864,256]{1,0:T(8,128)(2,1)S(1)} %broadcast_select_fusion.28), channel_id=1, source_target_pairs={{0,2},{2,0},{4,6},{6,4},{8,10},{10,8},{12,14},{14,12},{16,18},{18,... | collective-permute-start | bytes 1327112 | tf_op jit(solution)/shard_map/ppermute | solution.py:35
  1537.4 23.6 %collective-permute-start.76 = (bf16[864,256]{1,0:T(8,128)(2,1)S(1)}, bf16[864,256]{1,0:T(8,128)(2,1)S(1)}, u32[]{:S(2)}, u32[]{:S(2)}) collective-permute-start(bf16[864,256]{1,0:T(8,128)(2,1)S(1)} %broadcast_select_fusion.26), channel_id=1, source_target_pairs={{0,2},{2,0},{4,6},{6,4},{8,10},{10,8},{12,14},{14,12},{16,18},{18,... | collective-permute-start | bytes 1327112 | tf_op jit(solution)/shard_map/ppermute | solution.py:35
  1539.7 22.7 %collective-permute-start.102 = (bf16[864,256]{1,0:T(8,128)(2,1)S(1)}, bf16[864,256]{1,0:T(8,128)(2,1)S(1)}, u32[]{:S(2)}, u32[]{:S(2)}) collective-permute-start(bf16[864,256]{1,0:T(8,128)(2,1)S(1)} %broadcast_select_fusion.24), channel_id=1, source_target_pairs={{0,2},{2,0},{4,6},{6,4},{8,10},{10,8},{12,14},{14,12},{16,18},{18,... | collective-permute-start | bytes 1327112 | tf_op jit(solution)/shard_map/ppermute | solution.py:35
  1559.3 22.5 %collective-permute-start.51 = (bf16[864,2,256]{2,0,1:T(8,128)(2,1)S(1)}, bf16[864,2,256]{2,0,1:T(8,128)(2,1)S(1)}, u32[]{:S(2)}, u32[]{:S(2)}) collective-permute-start(bf16[864,2,256]{2,0,1:T(8,128)(2,1)S(1)} %pad_maximum_fusion.8), channel_id=1, source_target_pairs={{0,1},{1,0},{2,3},{3,2},{4,5},{5,4},{6,7},{7,6},{8,9},{9,8},{10,11... | collective-permute-start | bytes 2654216 | tf_op jit(solution)/shard_map/ppermute | solution.py:70
  1562.1 38.8 %collective-permute-start.77 = (bf16[864,2,256]{2,0,1:T(8,128)(2,1)}, bf16[864,2,256]{2,0,1:T(8,128)(2,1)}, u32[]{:S(2)}, u32[]{:S(2)}) collective-permute-start(bf16[864,2,256]{2,0,1:T(8,128)(2,1)} %pad_maximum_fusion.9), channel_id=1, source_target_pairs={{0,1},{1,0},{2,3},{3,2},{4,5},{5,4},{6,7},{7,6},{8,9},{9,8},{10,11... | collective-permute-start | bytes 2654216 | tf_op jit(solution)/shard_map/ppermute | solution.py:70
  1563.7 56.1 %collective-permute-start.103 = (bf16[864,2,256]{2,0,1:T(8,128)(2,1)}, bf16[864,2,256]{2,0,1:T(8,128)(2,1)}, u32[]{:S(2)}, u32[]{:S(2)}) collective-permute-start(bf16[864,2,256]{2,0,1:T(8,128)(2,1)} %pad_maximum_fusion.10), channel_id=1, source_target_pairs={{0,1},{1,0},{2,3},{3,2},{4,5},{5,4},{6,7},{7,6},{8,9},{9,8},{10,11... | collective-permute-start | bytes 2654216 | tf_op jit(solution)/shard_map/ppermute | solution.py:70
  1567.2 71.1 %collective-permute-start.129 = (bf16[864,2,256]{2,0,1:T(8,128)(2,1)}, bf16[864,2,256]{2,0,1:T(8,128)(2,1)}, u32[]{:S(2)}, u32[]{:S(2)}) collective-permute-start(bf16[864,2,256]{2,0,1:T(8,128)(2,1)} %pad_maximum_fusion.11), channel_id=1, source_target_pairs={{0,1},{1,0},{2,3},{3,2},{4,5},{5,4},{6,7},{7,6},{8,9},{9,8},{10,11... | collective-permute-start | bytes 2654216 | tf_op jit(solution)/shard_map/ppermute | solution.py:70
  (136 other events, 2064.8 us)
Sparse Core Ops, SparseCore 0:
  9.6 191.1 all-gather.3
  203.1 105.6 all-gather.5
  318.5 100.6 all-gather.7

commit v2 on v1

v2 whole, which is shorter than its diff:
```python
import jax
import jax.numpy as jnp
from jax import lax
from jax.experimental import pallas as pl
from jax.experimental.layout import Layout, with_layout_constraint
from jax.experimental.pallas import tpu as pltpu
from jax.sharding import PartitionSpec as P

SEQ = 256
EPSILON = 1e-05
BF = jnp.bfloat16
F32 = jnp.float32


def dot(left, right, dims):
    return lax.dot_general(left, right, (dims, ((), ())), preferred_element_type=F32)


def zero_after(array):
    first = lax.slice(array, (0,) * array.ndim, (1,) * array.ndim).reshape(())
    return jnp.minimum(jnp.abs(first.astype(F32)), 0.0)


def swap_core(array):
    wide = lax.axis_size("wide")
    return lax.ppermute(array, "wide", [(i, i ^ 1) for i in range(wide)])


def by_core(own, other):
    core = lax.axis_index("wide") % 2
    return jnp.where(core == 0, own, other), jnp.where(core == 0, other, own)


def plain(array):
    return with_layout_constraint(array, Layout(tuple(range(array.ndim))))


def join_core(array, other):
    core = lax.axis_index("wide") % 2
    out = plain(jnp.zeros((array.shape[0], 2) + array.shape[1:], array.dtype))
    out = lax.dynamic_update_slice_in_dim(out, array[:, None], core, 1)
    out = lax.dynamic_update_slice_in_dim(out, other[:, None], 1 - core, 1)
    return plain(out)


def swap_narrow(parts):
    if lax.axis_size("narrow") != 2:
        got = lax.all_to_all(jnp.stack(parts), "narrow", split_axis=0, concat_axis=0, tiled=True)
        return [got[n] for n in range(len(parts))]
    me = lax.axis_index("narrow")
    got = lax.ppermute(jnp.where(me == 0, parts[1], parts[0]), "narrow", [(0, 1), (1, 0)])
    return [jnp.where(me == 0, parts[0], got), jnp.where(me == 0, got, parts[1])]


def sum_narrow(parts):
    if lax.axis_size("narrow") != 2:
        return lax.psum_scatter(jnp.stack(parts), "narrow", scatter_dimension=0, tiled=True)[0]
    me = lax.axis_index("narrow")
    got = lax.ppermute(jnp.where(me == 0, parts[1], parts[0]), "narrow", [(0, 1), (1, 0)])
    return jnp.where(me == 0, parts[0], parts[1]) + got


def cut(array, count, axis):
    size = array.shape[axis] // count
    return [lax.slice_in_dim(array, n * size, (n + 1) * size, axis=axis) for n in range(count)]


def ring_chip(place, chips):
    lines = chips // 2
    return jnp.where(place < lines, 2 * place, 2 * (chips - 1 - place) + 1)


def ring_gather(block, odd):
    wide = lax.axis_size("wide")
    chips = wide // 2
    lines = chips // 2
    order = [2 * i if i < lines else 2 * (chips - 1 - i) + 1 for i in range(chips)]
    chip = lax.axis_index("wide") // 2
    place = jnp.where(chip % 2 == 0, chip // 2, chips - 1 - chip // 2)
    out = plain(jnp.zeros((chips,) + block.shape, block.dtype))
    out = lax.dynamic_update_slice_in_dim(out, block[None], chip, 0)
    many = chips // 2
    mark = last = block
    for step, hops in ((1, chips - 1 - many if odd else many), (-1, many if odd else chips - 1 - many)):
        pairs = [
            (2 * order[i] + core, 2 * order[(i + step) % chips] + core)
            for i in range(chips)
            for core in range(2)
        ]
        held = block
        for hop in range(1, hops + 1):
            held = lax.ppermute(held, "wide", pairs)
            source = ring_chip((place - step * hop) % chips, chips)
            out = lax.dynamic_update_slice_in_dim(out, held[None], source, 0)
            if hop == 2:
                mark = held
            last = held
    return plain(out), mark, last


def chip_exchange(array, axis, start):
    wide = lax.axis_size("wide")
    chips = wide // 2
    lines = chips // 2
    chip = lax.axis_index("wide") // 2
    line, side = chip // 2, chip % 2
    size = array.shape[axis] // chips
    shape = list(array.shape)
    shape[axis] = size
    out = plain(jnp.zeros([chips] + shape, array.dtype))
    for by_line in range(lines):
        for by_side in range(2):
            to = (line + by_line) % lines * 2 + (side + by_side) % 2
            piece = lax.dynamic_slice_in_dim(array, to * size + start, size, axis)
            if by_line or by_side:
                pairs = [
                    (2 * q + core, 2 * ((q // 2 + by_line) % lines * 2 + (q % 2 + by_side) % 2) + core)
                    for q in range(chips)
                    for core in range(2)
                ]
                piece = lax.ppermute(piece, "wide", pairs)
            source = (line - by_line) % lines * 2 + (side - by_side) % 2
            out = lax.dynamic_update_slice_in_dim(out, piece[None], source, 0)
    return plain(out)


def merge_stats(mine, got):
    largest = jnp.maximum(mine[0], got[0])
    a, b = jnp.exp(mine[0] - largest), jnp.exp(got[0] - largest)
    sums = mine[1:3] * a + got[1:3] * b
    return jnp.concatenate([largest[None], sums, mine[3:] + got[3:]])


def share_stats(stats):
    for axis in ("wide", "narrow"):
        count = lax.axis_size(axis)
        bit = 1
        while bit < count:
            got = lax.ppermute(stats, axis, [(i, i ^ bit) for i in range(count)])
            stats = merge_stats(stats, got)
            bit *= 2
    return stats


def square_kernel(samples, scale, first, inputs_ref, *refs):
    parts, out_ref = refs[:-1], refs[-1]
    total = 0.0
    if not first:
        total, parts = parts[0][...], parts[1:]
    for s in range(samples):
        pieces = []
        for part in parts:
            size = part.shape[1] // samples
            pieces.append(part[:, s * size : (s + 1) * size])
        left = jnp.concatenate(pieces, axis=1) if len(pieces) > 1 else pieces[0]
        block = dot(left, inputs_ref[...], ((1,), (1,)))
        total = total + block * block
    out_ref[...] = total if scale is None else total * scale


def add_squares(parts, inputs, total, samples, scale):
    rows, dirs = parts[0].shape[0], inputs.shape[0]
    row_block = 432 if rows % 432 == 0 else rows
    dir_block = 512 if dirs % 512 == 0 else dirs
    spec = pl.BlockSpec((row_block, dir_block), lambda i, j: (i, j))
    size = sum(part.shape[1] for part in parts)
    return pl.pallas_call(
        lambda *refs: square_kernel(samples, scale, total is None, *refs),
        out_shape=jax.ShapeDtypeStruct((rows, dirs), F32),
        grid=(rows // row_block, dirs // dir_block),
        in_specs=[pl.BlockSpec((dir_block, inputs.shape[1]), lambda i, j: (j, 0))]
        + ([] if total is None else [spec])
        + [pl.BlockSpec((row_block, part.shape[1]), lambda i, j: (i, 0)) for part in parts],
        out_specs=spec,
        input_output_aliases={1: 0} if total is not None and scale is None else {},
        compiler_params=pltpu.CompilerParams(vmem_limit_bytes=32 * 1024 * 1024),
        cost_estimate=pl.CostEstimate(
            flops=2 * rows * dirs * size,
            bytes_accessed=8 * rows * dirs + 2 * rows * size + 2 * inputs.size,
            transcendentals=0,
        ),
    )(inputs, *([] if total is None else [total]), *parts)


def per_device(
    resid, final_gain, unembed, labels, layer_in, gate_value, down_weight, basis_in, basis_out
):
    wide = lax.axis_size("wide")
    narrow = lax.axis_size("narrow")
    chips = wide // 2
    place = lax.axis_index("wide")
    chip, core = place // 2, place % 2
    narrow_place = lax.axis_index("narrow")
    own_tokens, width = resid.shape
    tokens, samples = labels.shape
    examples = tokens // SEQ
    cols = width // wide
    chip_cols = width // chips
    vocab_part = unembed.shape[0]
    vocab_own = vocab_part // wide
    hidden_part = down_weight.shape[0]
    hidden_own = hidden_part // chips
    half = SEQ // 2
    few = half // narrow
    group = 2 if examples % 2 == 0 else 1

    share = own_tokens // narrow
    mine = lax.dynamic_slice_in_dim(
        jnp.stack([resid, layer_in]), narrow_place * share, share, 1
    )
    ring, _, last = ring_gather(mine, 0)

    def all_tokens(part):
        rest = part.shape[2:]
        if narrow == 2:
            other = lax.ppermute(part, "narrow", [(0, 1), (1, 0)])
            out = plain(jnp.zeros((chips, 2) + part.shape[1:], part.dtype))
            out = lax.dynamic_update_slice_in_dim(out, part[:, None], narrow_place, 1)
            out = lax.dynamic_update_slice_in_dim(out, other[:, None], 1 - narrow_place, 1)
        else:
            out = lax.all_gather(part, "narrow", axis=1)
        out = out.reshape((chips, own_tokens) + rest)
        return join_core(out, swap_core(out)).reshape((tokens,) + rest)

    resid_all = all_tokens(ring[:, 0])
    layer_all = all_tokens(ring[:, 1] + zero_after(resid_all).astype(BF))

    unembed_own = lax.all_to_all(
        unembed.T + zero_after(last).astype(BF), "wide", split_axis=1, concat_axis=0, tiled=True
    )

    unembed_other = swap_core(unembed.T)
    basis_other = swap_core(basis_out.T)

    def own(array):
        array = array.reshape((examples, 2, narrow, few) + array.shape[1:])
        array = lax.dynamic_index_in_dim(array, core, 1, keepdims=False)
        return lax.dynamic_index_in_dim(array, narrow_place, 1, keepdims=False)

    def chip_columns(array):
        return jnp.concatenate(
            [
                lax.dynamic_slice_in_dim(array, (2 * chip + which) * cols, cols, array.ndim - 1)
                for which in (core, 1 - core)
            ],
            axis=-1,
        )

    order = lax.dynamic_index_in_dim(
        labels.reshape(examples, 2, narrow, few, samples), core, 1, keepdims=False
    )
    order = jnp.transpose(order, (1, 0, 3, 2)).reshape(-1)
    shifted = order - narrow_place * vocab_part
    inside = (shifted >= 0) & (shifted < vocab_part)
    shifted = jnp.clip(shifted, 0, vocab_part - 1)
    picked = [jnp.take(part, shifted, axis=0) for part in (unembed, unembed_other.T)]
    picked = jnp.concatenate(picked, axis=1)
    picked = jnp.where(inside[:, None], picked, jnp.zeros_like(picked))
    picked = sum_narrow(cut(picked, narrow, 0)).reshape(examples, samples, few, chip_cols)
    picked = jnp.transpose(picked, (0, 3, 1, 2))

    both = jnp.concatenate([down_weight.T, gate_value], axis=0)
    both = chip_exchange(both, 1, zero_after(unembed_own).astype(jnp.int32))
    down_own, gates = both[:, :cols], both[:, cols:]
    gates = join_core(gates, swap_core(gates))
    gates = gates.reshape(examples, 2, narrow, few, hidden_own)
    gates = lax.dynamic_index_in_dim(gates, core, 1, keepdims=False)
    gates = swap_narrow([jnp.transpose(gates[:, n], (0, 2, 1)) for n in range(narrow)])
    gates = jnp.concatenate(gates, axis=1)[:, :, None]

    basis_own = lax.all_to_all(
        basis_in + zero_after(both).astype(BF), "wide", split_axis=1, concat_axis=0, tiled=True
    )

    resid_float = resid_all.astype(F32)
    inverse = lax.rsqrt(jnp.mean(resid_float * resid_float, axis=1) + EPSILON)
    for array in (picked, basis_other, layer_all, basis_own, gates):
        inverse = inverse + zero_after(array)
    normed = (resid_float * inverse[:, None] * final_gain).astype(BF)
    logits = dot(unembed_own, normed, ((0,), (1,)))
    first_own = narrow_place * vocab_part + place * vocab_own
    entry = lax.broadcasted_iota(jnp.int32, logits.shape, 0) + first_own
    own_max = jnp.max(logits, axis=0)
    own_exp = jnp.exp(logits - own_max)
    stats = [own_max, jnp.sum(own_exp, axis=0), jnp.sum(own_exp * logits, axis=0)]
    for s in range(samples):
        stats.append(jnp.sum(jnp.where(entry == labels[:, s], logits, 0.0), axis=0))
    stats = share_stats(jnp.stack(stats))
    probs = (jnp.exp(logits - stats[0]) / stats[1]).astype(BF)
    inner = stats[2] / stats[1] - stats[3:]
    shrink = inner * (inverse * inverse / width)
    late = zero_after(stats)
    down_own = down_own + (zero_after(gates) + late).astype(BF)
    if narrow == 2:
        down_other = lax.ppermute(down_own, "narrow", [(0, 1), (1, 0)])

    probs = probs.reshape(vocab_own, examples, 2, half)
    keep = jnp.where(core == 0, probs[:, :, 0], probs[:, :, 1]).reshape(vocab_own, tokens // 2)
    give = jnp.where(core == 0, probs[:, :, 1], probs[:, :, 0]).reshape(vocab_own, tokens // 2)
    probs = jnp.concatenate(by_core(keep, swap_core(give)), axis=0)

    resid_cols = jnp.transpose(chip_columns(own(resid_all)), (0, 2, 1))
    inverse_own = own(inverse)
    shrink_own = jnp.transpose(own(shrink.T), (0, 2, 1))
    gain_cols = chip_columns(final_gain)

    inputs_own = (dot(basis_own, layer_all, ((0,), (1,))) + late).astype(BF)
    inputs_rot, _, _ = ring_gather(inputs_own, 1)
    inputs_rot = join_core(inputs_rot, swap_core(inputs_rot)).reshape(-1, tokens)
    dirs = inputs_rot.shape[0]

    def inputs_of(e):
        one = inputs_rot[:, e * SEQ : (e + 1) * SEQ]
        if narrow != 2:
            return one
        own_core, other_core = by_core(one[:, :half], one[:, half:])
        pieces = [cut(part, 2, 1) for part in (own_core, other_core)]
        mine = [jnp.where(narrow_place == 0, a, b) for a, b in pieces]
        rest = [jnp.where(narrow_place == 0, b, a) for a, b in pieces]
        return jnp.concatenate(mine + rest, axis=1)

    out_part = basis_out.shape[1]
    total = None
    backs = []
    start = jnp.float32(0)
    for g in range(examples // group):
        span = group * half
        probs_g = probs[:, g * span : (g + 1) * span] + start.astype(BF)
        probs_g, mark, _ = ring_gather(probs_g, g % 2)
        start = zero_after(mark)
        probs_g = probs_g.reshape(vocab_part, span)
        common = jnp.concatenate(
            [dot(part, probs_g, ((1,), (0,))) for part in (unembed.T, unembed_other)], axis=0
        )
        common = common.reshape(chip_cols, group, narrow, few)
        common = sum_narrow([common[:, :, n].reshape(chip_cols, group * few) for n in range(narrow)])
        back = []
        for i in range(group):
            e = g * group + i
            grads = common[:, None, i * few : (i + 1) * few] - picked[e].astype(F32)
            one = inverse_own[e] * gain_cols[:, None, None] * grads
            one = one - resid_cols[e].astype(F32)[:, None] * shrink_own[e]
            back.append(one.astype(BF).reshape(chip_cols, samples * few))
        back, _, _ = ring_gather(jnp.concatenate(back, axis=1), g % 2)
        backs += cut(back.reshape(width, -1), group, 1)
    if narrow == 2:
        down_other = down_other + start.astype(BF)
        down_own = jnp.concatenate(
            [
                jnp.where(narrow_place == 0, down_own, down_other),
                jnp.where(narrow_place == 0, down_other, down_own),
            ],
            axis=2,
        )
    else:
        down_own = lax.all_gather(down_own, "narrow", axis=2, tiled=True)
    down_own = jnp.stack([down_own, swap_core(down_own)], axis=1)
    down_own = down_own.reshape(width, narrow * hidden_own)

    starts = [jnp.float32(0)] * (examples + 2)
    ready = jnp.float32(0)
    for e in range(examples):
        hidden = dot(down_own, backs[e], ((0,), (0,)))
        hidden = hidden.reshape(narrow * hidden_own, samples, few)
        gated = (hidden * gates[e].astype(F32) + starts[e]).astype(BF)
        gated = gated.reshape(narrow * hidden_own, samples * few)
        gated = jnp.concatenate(swap_narrow(cut(gated, narrow, 0)), axis=1)
        gated, mark, _ = ring_gather(gated, e % 2)
        starts[e + 1] += zero_after(mark)
        gated = gated.reshape(hidden_part, narrow * samples * few)
        rotated = jnp.stack(
            [dot(part, gated, ((1,), (0,))) + ready for part in (basis_out.T, basis_other)]
        )
        ready = ready if total is None else zero_after(total)
        starts[e + 2] += zero_after(rotated)
        rotated = sum_narrow(cut(rotated, narrow, 2)).astype(BF)
        keep, got = rotated[0], swap_core(rotated[1])
        if narrow == 2:
            across = lax.ppermute(jnp.stack([keep, got]), "narrow", [(0, 1), (1, 0)])
            parts = [keep, got, across[0], across[1]]
        else:
            parts = jnp.stack(by_core(keep, got))
            parts = lax.all_gather(parts, "narrow", axis=0)
            parts = parts.reshape(narrow, 2, out_part, samples, few)
            parts = [jnp.transpose(parts, (2, 3, 1, 0, 4)).reshape(out_part, samples * SEQ)]
        scale = 1.0 / (examples * samples) if e == examples - 1 else None
        total = add_squares(parts, inputs_of(e), total, samples, scale)
    return total


def solution(mesh):
    in_specs = (
        P("wide", None),
        P(),
        P("narrow", "wide"),
        P(),
        P("wide", None),
        P("wide", "narrow"),
        P("narrow", "wide"),
        P("wide", "narrow"),
        P("narrow", "wide"),
    )
    out_specs = P("wide", "narrow")
    return jax.shard_map(
        per_device, mesh=mesh, in_specs=in_specs, out_specs=out_specs, check_vma=False
    )
```

time: 1730 us -> 1250 us (0.72)
  local copies, waits for them, and re-layouts: 557 us -> 297 us
  waiting for transfers between devices: 558 us -> 429 us
  starting transfers between devices: 263 us -> 197 us
    dynamic_update_slice x90 -> x80, local copies, waits for them, and re-layouts: 316 us -> 83.4 us  [the longest x70 56.9 us: ring_gather(): out = lax.dynamic_update_slice_in_dim(out, held[None], source, 0)]
    ppermute x84 -> x70, waiting for transfers between devices: 346 us -> 272 us  [ring_gather(): held = lax.ppermute(held, 'wide', pairs)]
    all_to_all x2, waiting for transfers between devices: 45.1 us -> 0.47 us  [the longest x1 0.47 us: per_device(): lax.all_to_all(basis_in + zero_after(both).astype(BF), 'wide', split_axis...]
    ppermute x28 -> x7, local copies, waits for them, and re-layouts: 50.3 us -> 10.7 us  [chip_exchange(): piece = lax.ppermute(piece, 'wide', pairs)]
    ppermute x5, waiting for transfers between devices: 0.01 us -> 33.9 us  [swap_narrow(): lax.ppermute(jnp.where(me == 0, parts[1], parts[0]), 'narrow', [(0, 1), (...]
    slice x4 -> x42, local copies, waits for them, and re-layouts: 6.05 us -> 37.6 us  [the longest x12 16.4 us: cut(): lax.slice_in_dim(array, n * size, (n + 1) * size, axis=axis)]
    transpose x11 -> x0, local copies, waits for them, and re-layouts: 30.9 us -> none  [the longest x4 20.2 us: per_device(): jnp.transpose(rotated, (0, 2, 1, 3)).reshape(out_part, samples * SEQ)]
    select_n x15 -> x16, other arithmetic: 44.6 us -> 17.1 us  [the longest x2 5.34 us: by_core(): return (jnp.where(core == 0, own, other), jnp.where(core == 0, other, own))]
  transfers between devices with their start and end apart: 135 -> 115, of which waited for: 78 -> 47; matrix products, arithmetic and copies ran while one was open for 47% -> 41% of each run, Pallas kernels for 0% -> 2%
where the time goes in v2:
time: 1250 us; the launch traced here: 1240 us
  waiting for transfers between devices  429 us (34%)
  local copies, waits for them, and re-layouts  297 us (24%)
  starting transfers between devices  197 us (16%)
  matrix products  145 us (12%)
  other arithmetic  122 us (10%)
  Pallas kernels  33.9 us (3%)
  between operations  15.1 us (1%)
    ppermute x70, waiting for transfers between devices, ring_gather(): held = lax.ppermute(held, 'wide', pairs)  272 us
    dot_general x18, matrix products, dot(): lax.dot_general(left, right, (dims, ((), ())), preferred_element_type=F32)  145 us
    ppermute x70, starting transfers between devices, ring_gather(): held = lax.ppermute(held, 'wide', pairs)  77.7 us
    ppermute x7, starting transfers between devices, chip_exchange(): piece = lax.ppermute(piece, 'wide', pairs)  57.7 us
    dynamic_update_slice x70, local copies, waits for them, and re-layouts, ring_gather(): out = lax.dynamic_update_slice_in_dim(out, held[None], source, 0)  56.9 us
    ppermute x2, waiting for transfers between devices, all_tokens(): other = lax.ppermute(part, 'narrow', [(0, 1), (1, 0)])  43.6 us
    unnamed x165, local copies, waits for them, and re-layouts  34.9 us
    ppermute x5, waiting for transfers between devices, swap_narrow(): lax.ppermute(jnp.where(me == 0, parts[1], parts[0]), 'narrow', [(0, 1), (...  33.9 us
  transfers between devices with their start and end apart: 115, of which 47 were waited for; matrix products, arithmetic and copies ran while one was open for 41% of the time, Pallas kernels for 2%

profile of v2, /device:TPU:0, one launch (start us, length us, event | category | flops | bytes accessed | tf_op | source)
XLA Modules:
  0.0 1239.6 jit_solution(3630701848653322552)
XLA Ops:
  7.0 14.6 %collective-permute-done.10 = bf16[2,32,5120]{2,1,0:T(8,128)(2,1)S(1)} collective-permute-done((bf16[2,32,5120]{2,1,0:T(8,128)(2,1)S(1)}, bf16[2,32,5120]{2,1,0:T(8,128)(2,1)S(1)}, u32[]{:S(2)}, u32[]{:S(2)}) %collective-permute-start.10) | collective-permute-done | bytes 655392 | tf_op jit(solution)/shard_map/ppermute | solution.py:92
  24.6 13.0 %collective-permute-done.11 = bf16[2,32,5120]{2,1,0:T(8,128)(2,1)S(1)} collective-permute-done((bf16[2,32,5120]{2,1,0:T(8,128)(2,1)S(1)}, bf16[2,32,5120]{2,1,0:T(8,128)(2,1)S(1)}, u32[]{:S(2)}, u32[]{:S(2)}) %collective-permute-start.11) | collective-permute-done | bytes 655392 | tf_op jit(solution)/shard_map/ppermute | solution.py:92
  40.5 12.1 collective-permute-done.12
  54.9 11.8 collective-permute-done.13
  85.1 6.3 all-to-all-start
  91.4 41.0 %collective-permute-done.14 = bf16[8,32,5120]{2,1,0:T(8,128)(2,1)} collective-permute-done((bf16[8,32,5120]{2,1,0:T(8,128)(2,1)S(1)}, bf16[8,32,5120]{2,1,0:T(8,128)(2,1)}, u32[]{:S(2)}, u32[]{:S(2)}) %collective-permute-start.14) | collective-permute-done | bytes 2621472 | tf_op jit(solution)/shard_map/ppermute | solution.py:216
  136.7 8.1 copy.112
  144.9 10.8 gather_fusion
  155.7 8.1 copy.113
  163.9 10.8 gather_fusion.1
  189.1 5.6 fusion.11
  198.1 7.6 copy.96
  218.7 5.5 fusion.19
  247.3 12.6 %collective-permute-done.5 = bf16[384,864]{0,1:T(8,128)(2,1)} collective-permute-done((bf16[384,864]{0,1:T(8,128)(2,1)}, bf16[384,864]{0,1:T(8,128)(2,1)}, u32[]{:S(2)}, u32[]{:S(2)}) %collective-permute-start.5) | collective-permute-done | bytes 663584 | tf_op jit(solution)/shard_map/ppermute | solution.py:121
  265.8 49.7 %collective-permute-start.9 = (bf16[384,864]{0,1:T(8,128)(2,1)}, bf16[384,864]{0,1:T(8,128)(2,1)}, u32[]{:S(2)}, u32[]{:S(2)}) collective-permute-start(bf16[384,864]{0,1:T(8,128)(2,1)} %get-tuple-element.42), channel_id=1, source_target_pairs={{0,28},{2,30},{4,24},{6,26},{8,4},{10,6},{12,0},{14,2},{16,12},{18... | collective-permute-start | bytes 1990664 | tf_op jit(solution)/shard_map/ppermute | solution.py:121
  339.4 20.7 %all-to-all-start.1 = ((bf16[320,16,160]{0,2,1:T(8,128)(2,1)}), bf16[320,16,160]{0,2,1:T(8,128)(2,1)S(1)}, u32[]{:S(2)}, u32[]{:S(2)}) async-start(bf16[320,16,160]{0,2,1:T(8,128)(2,1)} %bitcast.595), calls=%async_computation.1 | async-start | bytes 3932160 | tf_op jit(solution)/shard_map/all_to_all | solution.py:271
  374.4 6.1 fusion
  411.5 6.5 fusion.2
  418.1 7.7 fusion.76
  459.0 8.4 bitcast_dynamic-update-slice_fusion.97
  500.6 13.5 %collective-permute-done.30 = bf16[160,1024]{1,0:T(8,128)(2,1)S(1)} collective-permute-done((bf16[160,1024]{1,0:T(8,128)(2,1)S(1)}, bf16[160,1024]{1,0:T(8,128)(2,1)S(1)}, u32[]{:S(2)}, u32[]{:S(2)}) %collective-permute-start.30) | collective-permute-done | bytes 327712 | tf_op jit(solution)/shard_map/ppermute | solution.py:92
  520.4 7.2 collective-permute-done.44
  529.8 7.8 collective-permute-done.39
  544.4 7.4 collective-permute-done.40
  556.1 6.9 collective-permute-done.46
  586.3 7.5 collective-permute-done.48
  607.9 8.6 collective-permute-done.49
  622.8 8.5 fusion.59
  632.5 5.8 convolution_bitcast_fusion.5
  664.2 10.9 collective-permute-done.51
  680.2 9.0 collective-permute-done.84
  691.5 11.7 collective-permute-done.52
  711.3 8.4 pad_maximum_fusion
  722.6 6.9 fusion.6
  762.1 14.8 %collective-permute-done.61 = bf16[864,512]{1,0:T(8,128)(2,1)} collective-permute-done((bf16[864,512]{1,0:T(8,128)(2,1)}, bf16[864,512]{1,0:T(8,128)(2,1)}, u32[]{:S(2)}, u32[]{:S(2)}) %collective-permute-start.61) | collective-permute-done | bytes 884768 | tf_op jit(solution)/shard_map/ppermute | solution.py:92
  784.5 6.3 collective-permute-done.90
  793.8 13.5 %collective-permute-done.62 = bf16[864,512]{1,0:T(8,128)(2,1)S(1)} collective-permute-done((bf16[864,512]{1,0:T(8,128)(2,1)}, bf16[864,512]{1,0:T(8,128)(2,1)S(1)}, u32[]{:S(2)}, u32[]{:S(2)}) %collective-permute-start.62) | collective-permute-done | bytes 884768 | tf_op jit(solution)/shard_map/ppermute | solution.py:92
  808.5 9.0 fusion.7
  853.4 12.7 %collective-permute-done.71 = bf16[864,512]{1,0:T(8,128)(2,1)S(1)} collective-permute-done((bf16[864,512]{1,0:T(8,128)(2,1)S(1)}, bf16[864,512]{1,0:T(8,128)(2,1)S(1)}, u32[]{:S(2)}, u32[]{:S(2)}) %collective-permute-start.71) | collective-permute-done | bytes 884768 | tf_op jit(solution)/shard_map/ppermute | solution.py:92
  868.5 16.7 %collective-permute-done.60 = bf16[864,512]{1,0:T(8,128)(2,1)S(1)} collective-permute-done((bf16[864,512]{1,0:T(8,128)(2,1)}, bf16[864,512]{1,0:T(8,128)(2,1)S(1)}, u32[]{:S(2)}, u32[]{:S(2)}) %collective-permute-start.60) | collective-permute-done | bytes 884768 | tf_op jit(solution)/shard_map/ppermute | solution.py:92
  886.8 8.8 convolution_bitcast_fusion.3
  895.6 9.4 convolution_bitcast_fusion.2
  911.1 11.9 fusion.8
  932.7 20.3 %collective-permute-done.91 = bf16[864,256]{1,0:T(8,128)(2,1)S(1)} collective-permute-done((bf16[864,256]{1,0:T(8,128)(2,1)S(1)}, bf16[864,256]{1,0:T(8,128)(2,1)S(1)}, u32[]{:S(2)}, u32[]{:S(2)}) %collective-permute-start.91) | collective-permute-done | bytes 442400 | tf_op jit(solution)/shard_map/ppermute | solution.py:51
  962.4 13.4 %collective-permute-done.96 = bf16[864,512]{1,0:T(8,128)(2,1)S(1)} collective-permute-done((bf16[864,512]{1,0:T(8,128)(2,1)S(1)}, bf16[864,512]{1,0:T(8,128)(2,1)S(1)}, u32[]{:S(2)}, u32[]{:S(2)}) %collective-permute-start.96) | collective-permute-done | bytes 884768 | tf_op jit(solution)/shard_map/ppermute | solution.py:92
  979.6 15.2 %collective-permute-done.74 = bf16[864,512]{1,0:T(8,128)(2,1)S(1)} collective-permute-done((bf16[864,512]{1,0:T(8,128)(2,1)S(1)}, bf16[864,512]{1,0:T(8,128)(2,1)S(1)}, u32[]{:S(2)}, u32[]{:S(2)}) %collective-permute-start.74) | collective-permute-done | bytes 884768 | tf_op jit(solution)/shard_map/ppermute | solution.py:92
  994.8 8.8 convolution_bitcast_fusion.1
  1003.7 9.4 convolution_bitcast_fusion
  1018.6 11.9 fusion.9
  1044.7 8.0 collective-permute-done.102
  1057.1 7.5 shard_map.91.refs_1_
  1072.0 11.4 collective-permute-done.103
  1088.4 10.9 collective-permute-done.95
  1100.9 8.8 add_bitcast_fusion.3
  1109.7 8.8 add_bitcast_fusion.2
  1124.4 8.5 shard_map.92.refs_1_
  1138.0 9.4 collective-permute-done.109
  1147.4 8.8 add_bitcast_fusion.1
  1156.3 8.8 add_bitcast_fusion
  1169.1 18.9 %collective-permute-done.110 = f32[2,864,256]{2,1,0:T(8,128)S(1)} collective-permute-done((f32[2,864,256]{2,1,0:T(8,128)S(1)}, f32[2,864,256]{2,1,0:T(8,128)S(1)}, u32[]{:S(2)}, u32[]{:S(2)}) %collective-permute-start.110) | collective-permute-done | bytes 1769504 | tf_op jit(solution)/shard_map/ppermute | solution.py:59
  1193.4 17.8 %collective-permute-done.101 = bf16[2,864,256]{2,1,0:T(8,128)(2,1)S(1)} collective-permute-done((bf16[2,864,256]{2,1,0:T(8,128)(2,1)S(1)}, bf16[2,864,256]{2,1,0:T(8,128)(2,1)S(1)}, u32[]{:S(2)}, u32[]{:S(2)}) %collective-permute-start.101) | collective-permute-done | bytes 884768 | tf_op jit(solution)/shard_map/ppermute | solution.py:379
  1211.3 8.6 shard_map.93.refs_1_
  1219.9 10.1 collective-permute-done.112
  1230.1 9.3 shard_map.94
  (690 shorter events, 499.6 us)
Async XLA Ops:
  39.1 30.2 %collective-permute-start.2 = (bf16[2,32,5120]{2,1,0:T(8,128)(2,1)S(1)}, bf16[2,32,5120]{2,1,0:T(8,128)(2,1)S(1)}, u32[]{:S(2)}, u32[]{:S(2)}) collective-permute-start(bf16[2,32,5120]{2,1,0:T(8,128)(2,1)S(1)} %collective-permute-done.1), channel_id=1, source_target_pairs={{0,4},{2,6},{8,0},{10,2},{16,8},{18,10},{24,16},{26,18},{28,24},{3... | collective-permute-start | bytes 1966088 | tf_op jit(solution)/shard_map/ppermute | solution.py:92
  77.0 55.4 %collective-permute-start.14 = (bf16[8,32,5120]{2,1,0:T(8,128)(2,1)S(1)}, bf16[8,32,5120]{2,1,0:T(8,128)(2,1)}, u32[]{:S(2)}, u32[]{:S(2)}) collective-permute-start(bf16[8,32,5120]{2,1,0:T(8,128)(2,1)S(1)} %get-tuple-element.64), channel_id=1, source_target_pairs={{0,1},{1,0},{2,3},{3,2},{4,5},{5,4},{6,7},{7,6},{8,9},{9,8},{10,11... | collective-permute-start | bytes 7864328 | tf_op jit(solution)/shard_map/ppermute | solution.py:216
  78.2 77.5 %collective-permute-start.18 = (bf16[320,8192]{1,0:T(8,128)(2,1)}, bf16[320,8192]{1,0:T(8,128)(2,1)}, u32[]{:S(2)}, u32[]{:S(2)}) collective-permute-start(bf16[320,8192]{1,0:T(8,128)(2,1)} %bitcast.1), channel_id=1, source_target_pairs={{0,2},{2,0},{4,6},{6,4},{8,10},{10,8},{12,14},{14,12},{16,18},{18,... | collective-permute-start | bytes 15728648 | tf_op jit(solution)/shard_map/ppermute | solution.py:26
  85.1 131.8 %all-to-all-start = ((bf16[320,16,512]{2,0,1:T(8,128)(2,1)}), bf16[320,16,512]{2,0,1:T(8,128)(2,1)}, u32[]{:S(2)}, u32[]{:S(2)}) async-start(bf16[320,16,512]{2,0,1:T(8,128)(2,1)} %bitcast.577), calls=%async_computation | async-start | bytes 10485760 | tf_op jit(solution)/shard_map/all_to_all | solution.py:228
  135.8 48.1 %collective-permute-start.15 = (bf16[8,64,5120]{2,1,0:T(8,128)(2,1)}, bf16[8,64,5120]{2,1,0:T(8,128)(2,1)}, u32[]{:S(2)}, u32[]{:S(2)}) collective-permute-start(bf16[8,64,5120]{2,1,0:T(8,128)(2,1)} %bitcast.32), channel_id=1, source_target_pairs={{0,2},{2,0},{4,6},{6,4},{8,10},{10,8},{12,14},{14,12},{16,18},{18,... | collective-permute-start | bytes 15728648 | tf_op jit(solution)/shard_map/ppermute | solution.py:26
  135.8 244.7 %collective-permute-start.20 = (bf16[864,6912]{1,0:T(8,128)(2,1)}, bf16[864,6912]{1,0:T(8,128)(2,1)}, u32[]{:S(2)}, u32[]{:S(2)}) collective-permute-start(bf16[864,6912]{1,0:T(8,128)(2,1)} %bitcast.688), channel_id=1, source_target_pairs={{0,2},{2,0},{4,6},{6,4},{8,10},{10,8},{12,14},{14,12},{16,18},{18,... | collective-permute-start | bytes 35831816 | tf_op jit(solution)/shard_map/ppermute | solution.py:26
  178.6 34.8 %collective-permute-start.19 = (bf16[1024,640]{1,0:T(8,128)(2,1)}, bf16[1024,640]{1,0:T(8,128)(2,1)}, u32[]{:S(2)}, u32[]{:S(2)}) collective-permute-start(bf16[1024,640]{1,0:T(8,128)(2,1)} %broadcast_select_fusion.4), channel_id=1, source_target_pairs={{0,1},{1,0},{2,3},{3,2},{4,5},{5,4},{6,7},{7,6},{8,9},{9,8},{10,11... | collective-permute-start | bytes 3932168 | tf_op jit(solution)/shard_map/ppermute | solution.py:59
  197.0 68.8 %collective-permute-start.16 = (bf16[8,32,5120]{2,1,0:T(8,128)(2,1)}, bf16[8,32,5120]{2,1,0:T(8,128)(2,1)}, u32[]{:S(2)}, u32[]{:S(2)}) collective-permute-start(bf16[8,32,5120]{2,1,0:T(8,128)(2,1)} %get-tuple-element.62), channel_id=1, source_target_pairs={{0,1},{1,0},{2,3},{3,2},{4,5},{5,4},{6,7},{7,6},{8,9},{9,8},{10,11... | collective-permute-start | bytes 7864328 | tf_op jit(solution)/shard_map/ppermute | solution.py:216
  226.8 33.2 %collective-permute-start.5 = (bf16[384,864]{0,1:T(8,128)(2,1)}, bf16[384,864]{0,1:T(8,128)(2,1)}, u32[]{:S(2)}, u32[]{:S(2)}) collective-permute-start(bf16[384,864]{0,1:T(8,128)(2,1)} %get-tuple-element.46), channel_id=1, source_target_pairs={{0,12},{2,14},{4,8},{6,10},{8,20},{10,22},{12,16},{14,18},{16,28},... | collective-permute-start | bytes 1990664 | tf_op jit(solution)/shard_map/ppermute | solution.py:121
  240.8 78.1 %collective-permute-start.7 = (bf16[384,864]{0,1:T(8,128)(2,1)}, bf16[384,864]{0,1:T(8,128)(2,1)S(1)}, u32[]{:S(2)}, u32[]{:S(2)}) collective-permute-start(bf16[384,864]{0,1:T(8,128)(2,1)} %get-tuple-element.49), channel_id=1, source_target_pairs={{0,20},{2,22},{4,16},{6,18},{8,28},{10,30},{12,24},{14,26},{16,4},... | collective-permute-start | bytes 1990664 | tf_op jit(solution)/shard_map/ppermute | solution.py:121
  245.8 74.3 %collective-permute-start.6 = (bf16[384,864]{0,1:T(8,128)(2,1)}, bf16[384,864]{0,1:T(8,128)(2,1)}, u32[]{:S(2)}, u32[]{:S(2)}) collective-permute-start(bf16[384,864]{0,1:T(8,128)(2,1)} %get-tuple-element.47), channel_id=1, source_target_pairs={{0,16},{2,18},{4,20},{6,22},{8,24},{10,26},{12,28},{14,30},{16,0},... | collective-permute-start | bytes 1990664 | tf_op jit(solution)/shard_map/ppermute | solution.py:121
  260.0 62.4 %collective-permute-start.8 = (bf16[384,864]{0,1:T(8,128)(2,1)}, bf16[384,864]{0,1:T(8,128)(2,1)}, u32[]{:S(2)}, u32[]{:S(2)}) collective-permute-start(bf16[384,864]{0,1:T(8,128)(2,1)} %get-tuple-element.48), channel_id=1, source_target_pairs={{0,24},{2,26},{4,28},{6,30},{8,0},{10,2},{12,4},{14,6},{16,8},{18,... | collective-permute-start | bytes 1990664 | tf_op jit(solution)/shard_map/ppermute | solution.py:121
  265.8 63.3 %collective-permute-start.9 = (bf16[384,864]{0,1:T(8,128)(2,1)}, bf16[384,864]{0,1:T(8,128)(2,1)}, u32[]{:S(2)}, u32[]{:S(2)}) collective-permute-start(bf16[384,864]{0,1:T(8,128)(2,1)} %get-tuple-element.42), channel_id=1, source_target_pairs={{0,28},{2,30},{4,24},{6,26},{8,4},{10,6},{12,0},{14,2},{16,12},{18... | collective-permute-start | bytes 1990664 | tf_op jit(solution)/shard_map/ppermute | solution.py:121
  318.8 85.6 %collective-permute-start.17 = (bf16[8,64,5120]{2,1,0:T(8,128)(2,1)}, bf16[8,64,5120]{2,1,0:T(8,128)(2,1)}, u32[]{:S(2)}, u32[]{:S(2)}) collective-permute-start(bf16[8,64,5120]{2,1,0:T(8,128)(2,1)} %bitcast.578), channel_id=1, source_target_pairs={{0,2},{2,0},{4,6},{6,4},{8,10},{10,8},{12,14},{14,12},{16,18},{18,... | collective-permute-start | bytes 15728648 | tf_op jit(solution)/shard_map/ppermute | solution.py:26
  339.4 59.5 %all-to-all-start.1 = ((bf16[320,16,160]{0,2,1:T(8,128)(2,1)}), bf16[320,16,160]{0,2,1:T(8,128)(2,1)S(1)}, u32[]{:S(2)}, u32[]{:S(2)}) async-start(bf16[320,16,160]{0,2,1:T(8,128)(2,1)} %bitcast.595), calls=%async_computation.1 | async-start | bytes 3932160 | tf_op jit(solution)/shard_map/all_to_all | solution.py:271
  485.2 133.3 %collective-permute-start.36 = (bf16[8,320,864]{2,1,0:T(8,128)(2,1)}, bf16[8,320,864]{2,1,0:T(8,128)(2,1)}, u32[]{:S(2)}, u32[]{:S(2)}) collective-permute-start(bf16[8,320,864]{2,1,0:T(8,128)(2,1)} %slice_add_fusion), channel_id=1, source_target_pairs={{0,1},{1,0},{2,3},{3,2},{4,5},{5,4},{6,7},{7,6},{8,9},{9,8},{10,11... | collective-permute-start | bytes 13271048 | tf_op jit(solution)/shard_map/ppermute | solution.py:295
  489.4 24.8 %collective-permute-start.43 = (bf16[1024,256]{1,0:T(8,128)(2,1)S(1)}, bf16[1024,256]{1,0:T(8,128)(2,1)S(1)}, u32[]{:S(2)}, u32[]{:S(2)}) collective-permute-start(bf16[1024,256]{1,0:T(8,128)(2,1)S(1)} %get-tuple-element.23), channel_id=1, source_target_pairs={{0,8},{2,10},{8,16},{10,18},{16,24},{18,26},{24,28},{26,30},{28,20... | collective-permute-start | bytes 1572872 | tf_op jit(solution)/shard_map/ppermute | solution.py:92
  529.7 115.6 %collective-permute-start.35 = (bf16[8,160,1024]{2,1,0:T(8,128)(2,1)S(1)}, bf16[8,160,1024]{2,1,0:T(8,128)(2,1)}, u32[]{:S(2)}, u32[]{:S(2)}) collective-permute-start(bf16[8,160,1024]{2,1,0:T(8,128)(2,1)S(1)} %bitcast_dynamic-update-slice_fusion.90), channel_id=1, source_target_pairs={{0,2},{2,0},{4,6},{6,4},{8,10},{10,8},{12,14},{14,12},{16,18},{18,... | collective-permute-start | bytes 7864328 | tf_op jit(solution)/shard_map/ppermute | solution.py:26
  555.2 25.3 %collective-permute-start.41 = (bf16[1024,256]{1,0:T(8,128)(2,1)}, bf16[1024,256]{1,0:T(8,128)(2,1)}, u32[]{:S(2)}, u32[]{:S(2)}) collective-permute-start(bf16[1024,256]{1,0:T(8,128)(2,1)} %collective-permute-done.40), channel_id=1, source_target_pairs={{0,4},{2,6},{8,0},{10,2},{16,8},{18,10},{24,16},{26,18},{28,24},{3... | collective-permute-start | bytes 1572872 | tf_op jit(solution)/shard_map/ppermute | solution.py:92
  602.5 29.9 %collective-permute-start.53 = (bf16[640,512]{1,0:T(8,128)(2,1)S(1)}, bf16[640,512]{1,0:T(8,128)(2,1)}, u32[]{:S(2)}, u32[]{:S(2)}) collective-permute-start(bf16[640,512]{1,0:T(8,128)(2,1)S(1)} %pad_maximum_fusion.20), channel_id=1, source_target_pairs={{0,4},{2,6},{8,0},{10,2},{16,8},{18,10},{24,16},{26,18},{28,24},{3... | collective-permute-start | bytes 1966088 | tf_op jit(solution)/shard_map/ppermute | solution.py:92
  602.6 29.9 %collective-permute-start.82 = (bf16[1024,256]{1,0:T(8,128)(2,1)}, bf16[1024,256]{1,0:T(8,128)(2,1)S(1)}, u32[]{:S(2)}, u32[]{:S(2)}) collective-permute-start(bf16[1024,256]{1,0:T(8,128)(2,1)} %collective-permute-done.81), channel_id=1, source_target_pairs={{0,4},{2,6},{8,0},{10,2},{16,8},{18,10},{24,16},{26,18},{28,24},{3... | collective-permute-start | bytes 1572872 | tf_op jit(solution)/shard_map/ppermute | solution.py:92
  616.4 40.9 %collective-permute-start.50 = (bf16[640,512]{1,0:T(8,128)(2,1)}, bf16[640,512]{1,0:T(8,128)(2,1)}, u32[]{:S(2)}, u32[]{:S(2)}) collective-permute-start(bf16[640,512]{1,0:T(8,128)(2,1)} %collective-permute-done.49), channel_id=1, source_target_pairs={{0,8},{2,10},{8,16},{10,18},{16,24},{18,26},{24,28},{26,30},{28,20... | collective-permute-start | bytes 1966088 | tf_op jit(solution)/shard_map/ppermute | solution.py:92
  631.2 80.0 %collective-permute-start.42 = (bf16[8,320,1728]{2,1,0:T(8,128)(2,1)}, bf16[8,320,1728]{2,1,0:T(8,128)(2,1)}, u32[]{:S(2)}, u32[]{:S(2)}) collective-permute-start(bf16[8,320,1728]{2,1,0:T(8,128)(2,1)} %get-tuple-element.39), channel_id=1, source_target_pairs={{0,2},{2,0},{4,6},{6,4},{8,10},{10,8},{12,14},{14,12},{16,18},{18,... | collective-permute-start | bytes 26542088 | tf_op jit(solution)/shard_map/ppermute | solution.py:26
  632.4 44.9 %collective-permute-start.54 = (bf16[640,512]{1,0:T(8,128)(2,1)}, bf16[640,512]{1,0:T(8,128)(2,1)}, u32[]{:S(2)}, u32[]{:S(2)}) collective-permute-start(bf16[640,512]{1,0:T(8,128)(2,1)} %collective-permute-done.53), channel_id=1, source_target_pairs={{0,4},{2,6},{8,0},{10,2},{16,8},{18,10},{24,16},{26,18},{28,24},{3... | collective-permute-start | bytes 1966088 | tf_op jit(solution)/shard_map/ppermute | solution.py:92
  662.2 27.0 %collective-permute-start.84 = (bf16[640,512]{1,0:T(8,128)(2,1)S(1)}, bf16[640,512]{1,0:T(8,128)(2,1)}, u32[]{:S(2)}, u32[]{:S(2)}) collective-permute-start(bf16[640,512]{1,0:T(8,128)(2,1)S(1)} %pad_maximum_fusion.22), channel_id=1, source_target_pairs={{0,8},{2,10},{8,16},{10,18},{16,24},{18,26},{24,28},{26,30},{28,20... | collective-permute-start | bytes 1966088 | tf_op jit(solution)/shard_map/ppermute | solution.py:92
  664.1 25.4 %collective-permute-start.87 = (bf16[640,512]{1,0:T(8,128)(2,1)S(1)}, bf16[640,512]{1,0:T(8,128)(2,1)}, u32[]{:S(2)}, u32[]{:S(2)}) collective-permute-start(bf16[640,512]{1,0:T(8,128)(2,1)S(1)} %pad_maximum_fusion.22), channel_id=1, source_target_pairs={{0,4},{2,6},{8,0},{10,2},{16,8},{18,10},{24,16},{26,18},{28,24},{3... | collective-permute-start | bytes 1966088 | tf_op jit(solution)/shard_map/ppermute | solution.py:92
  675.1 28.1 %collective-permute-start.52 = (bf16[640,512]{1,0:T(8,128)(2,1)S(1)}, bf16[640,512]{1,0:T(8,128)(2,1)S(1)}, u32[]{:S(2)}, u32[]{:S(2)}) collective-permute-start(bf16[640,512]{1,0:T(8,128)(2,1)S(1)} %collective-permute-done.51), channel_id=1, source_target_pairs={{0,8},{2,10},{8,16},{10,18},{16,24},{18,26},{24,28},{26,30},{28,20... | collective-permute-start | bytes 1966088 | tf_op jit(solution)/shard_map/ppermute | solution.py:92
  677.3 28.2 %collective-permute-start.55 = (bf16[640,512]{1,0:T(8,128)(2,1)}, bf16[640,512]{1,0:T(8,128)(2,1)S(1)}, u32[]{:S(2)}, u32[]{:S(2)}) collective-permute-start(bf16[640,512]{1,0:T(8,128)(2,1)} %collective-permute-done.54), channel_id=1, source_target_pairs={{0,4},{2,6},{8,0},{10,2},{16,8},{18,10},{24,16},{26,18},{28,24},{3... | collective-permute-start | bytes 1966088 | tf_op jit(solution)/shard_map/ppermute | solution.py:92
  689.2 50.4 %collective-permute-start.85 = (bf16[640,512]{1,0:T(8,128)(2,1)}, bf16[640,512]{1,0:T(8,128)(2,1)}, u32[]{:S(2)}, u32[]{:S(2)}) collective-permute-start(bf16[640,512]{1,0:T(8,128)(2,1)} %collective-permute-done.84), channel_id=1, source_target_pairs={{0,8},{2,10},{8,16},{10,18},{16,24},{18,26},{24,28},{26,30},{28,20... | collective-permute-start | bytes 1966088 | tf_op jit(solution)/shard_map/ppermute | solution.py:92
  689.5 50.4 %collective-permute-start.88 = (bf16[640,512]{1,0:T(8,128)(2,1)}, bf16[640,512]{1,0:T(8,128)(2,1)}, u32[]{:S(2)}, u32[]{:S(2)}) collective-permute-start(bf16[640,512]{1,0:T(8,128)(2,1)} %collective-permute-done.87), channel_id=1, source_target_pairs={{0,4},{2,6},{8,0},{10,2},{16,8},{18,10},{24,16},{26,18},{28,24},{3... | collective-permute-start | bytes 1966088 | tf_op jit(solution)/shard_map/ppermute | solution.py:92
  745.6 31.3 %collective-permute-start.61 = (bf16[864,512]{1,0:T(8,128)(2,1)}, bf16[864,512]{1,0:T(8,128)(2,1)}, u32[]{:S(2)}, u32[]{:S(2)}) collective-permute-start(bf16[864,512]{1,0:T(8,128)(2,1)} %pad_maximum_fusion.11), channel_id=1, source_target_pairs={{0,4},{2,6},{8,0},{10,2},{16,8},{18,10},{24,16},{26,18},{28,24},{3... | collective-permute-start | bytes 2654216 | tf_op jit(solution)/shard_map/ppermute | solution.py:92
  757.9 32.9 %collective-permute-start.90 = (bf16[640,512]{1,0:T(8,128)(2,1)}, bf16[640,512]{1,0:T(8,128)(2,1)S(1)}, u32[]{:S(2)}, u32[]{:S(2)}) collective-permute-start(bf16[640,512]{1,0:T(8,128)(2,1)} %collective-permute-done.89), channel_id=1, source_target_pairs={{0,4},{2,6},{8,0},{10,2},{16,8},{18,10},{24,16},{26,18},{28,24},{3... | collective-permute-start | bytes 1966088 | tf_op jit(solution)/shard_map/ppermute | solution.py:92
  761.7 30.0 %collective-permute-start.57 = (bf16[864,512]{1,0:T(8,128)(2,1)}, bf16[864,512]{1,0:T(8,128)(2,1)}, u32[]{:S(2)}, u32[]{:S(2)}) collective-permute-start(bf16[864,512]{1,0:T(8,128)(2,1)} %pad_maximum_fusion.11), channel_id=1, source_target_pairs={{0,8},{2,10},{8,16},{10,18},{16,24},{18,26},{24,28},{26,30},{28,20... | collective-permute-start | bytes 2654216 | tf_op jit(solution)/shard_map/ppermute | solution.py:92
  776.9 30.4 %collective-permute-start.62 = (bf16[864,512]{1,0:T(8,128)(2,1)}, bf16[864,512]{1,0:T(8,128)(2,1)S(1)}, u32[]{:S(2)}, u32[]{:S(2)}) collective-permute-start(bf16[864,512]{1,0:T(8,128)(2,1)} %collective-permute-done.61), channel_id=1, source_target_pairs={{0,4},{2,6},{8,0},{10,2},{16,8},{18,10},{24,16},{26,18},{28,24},{3... | collective-permute-start | bytes 2654216 | tf_op jit(solution)/shard_map/ppermute | solution.py:92
  791.7 33.6 %collective-permute-start.58 = (bf16[864,512]{1,0:T(8,128)(2,1)}, bf16[864,512]{1,0:T(8,128)(2,1)}, u32[]{:S(2)}, u32[]{:S(2)}) collective-permute-start(bf16[864,512]{1,0:T(8,128)(2,1)} %collective-permute-done.57), channel_id=1, source_target_pairs={{0,8},{2,10},{8,16},{10,18},{16,24},{18,26},{24,28},{26,30},{28,20... | collective-permute-start | bytes 2654216 | tf_op jit(solution)/shard_map/ppermute | solution.py:92
  843.4 22.6 %collective-permute-start.71 = (bf16[864,512]{1,0:T(8,128)(2,1)S(1)}, bf16[864,512]{1,0:T(8,128)(2,1)S(1)}, u32[]{:S(2)}, u32[]{:S(2)}) collective-permute-start(bf16[864,512]{1,0:T(8,128)(2,1)S(1)} %pad_maximum_fusion.13), channel_id=1, source_target_pairs={{0,4},{2,6},{8,0},{10,2},{16,8},{18,10},{24,16},{26,18},{28,24},{3... | collective-permute-start | bytes 2654216 | tf_op jit(solution)/shard_map/ppermute | solution.py:92
  843.7 22.7 %collective-permute-start.68 = (bf16[864,512]{1,0:T(8,128)(2,1)S(1)}, bf16[864,512]{1,0:T(8,128)(2,1)}, u32[]{:S(2)}, u32[]{:S(2)}) collective-permute-start(bf16[864,512]{1,0:T(8,128)(2,1)S(1)} %pad_maximum_fusion.13), channel_id=1, source_target_pairs={{0,8},{2,10},{8,16},{10,18},{16,24},{18,26},{24,28},{26,30},{28,20... | collective-permute-start | bytes 2654216 | tf_op jit(solution)/shard_map/ppermute | solution.py:92
  846.2 39.1 %collective-permute-start.60 = (bf16[864,512]{1,0:T(8,128)(2,1)}, bf16[864,512]{1,0:T(8,128)(2,1)S(1)}, u32[]{:S(2)}, u32[]{:S(2)}) collective-permute-start(bf16[864,512]{1,0:T(8,128)(2,1)} %collective-permute-done.59), channel_id=1, source_target_pairs={{0,8},{2,10},{8,16},{10,18},{16,24},{18,26},{24,28},{26,30},{28,20... | collective-permute-start | bytes 2654216 | tf_op jit(solution)/shard_map/ppermute | solution.py:92
  849.0 37.7 %collective-permute-start.63 = (bf16[864,512]{1,0:T(8,128)(2,1)S(1)}, bf16[864,512]{1,0:T(8,128)(2,1)S(1)}, u32[]{:S(2)}, u32[]{:S(2)}) collective-permute-start(bf16[864,512]{1,0:T(8,128)(2,1)S(1)} %copy-done.57), channel_id=1, source_target_pairs={{0,4},{2,6},{8,0},{10,2},{16,8},{18,10},{24,16},{26,18},{28,24},{3... | collective-permute-start | bytes 2654216 | tf_op jit(solution)/shard_map/ppermute | solution.py:92
  866.0 42.8 %collective-permute-start.72 = (bf16[864,512]{1,0:T(8,128)(2,1)S(1)}, bf16[864,512]{1,0:T(8,128)(2,1)S(1)}, u32[]{:S(2)}, u32[]{:S(2)}) collective-permute-start(bf16[864,512]{1,0:T(8,128)(2,1)S(1)} %collective-permute-done.71), channel_id=1, source_target_pairs={{0,4},{2,6},{8,0},{10,2},{16,8},{18,10},{24,16},{26,18},{28,24},{3... | collective-permute-start | bytes 2654216 | tf_op jit(solution)/shard_map/ppermute | solution.py:92
  866.4 61.5 %collective-permute-start.69 = (bf16[864,512]{1,0:T(8,128)(2,1)}, bf16[864,512]{1,0:T(8,128)(2,1)}, u32[]{:S(2)}, u32[]{:S(2)}) collective-permute-start(bf16[864,512]{1,0:T(8,128)(2,1)} %collective-permute-done.68), channel_id=1, source_target_pairs={{0,8},{2,10},{8,16},{10,18},{16,24},{18,26},{24,28},{26,30},{28,20... | collective-permute-start | bytes 2654216 | tf_op jit(solution)/shard_map/ppermute | solution.py:92
  907.7 49.6 %collective-permute-start.64 = (f32[2,864,256]{2,1,0:T(8,128)}, f32[2,864,256]{2,1,0:T(8,128)}, u32[]{:S(2)}, u32[]{:S(2)}) collective-permute-start(f32[2,864,256]{2,1,0:T(8,128)} %broadcast_select_fusion.8), channel_id=1, source_target_pairs={{0,1},{1,0},{2,3},{3,2},{4,5},{5,4},{6,7},{7,6},{8,9},{9,8},{10,11... | collective-permute-start | bytes 5308424 | tf_op jit(solution)/shard_map/ppermute | solution.py:59
  925.4 27.6 %collective-permute-start.91 = (bf16[864,256]{1,0:T(8,128)(2,1)S(1)}, bf16[864,256]{1,0:T(8,128)(2,1)S(1)}, u32[]{:S(2)}, u32[]{:S(2)}) collective-permute-start(bf16[864,256]{1,0:T(8,128)(2,1)S(1)} %broadcast_select_fusion.43), channel_id=1, source_target_pairs={{0,1},{1,0},{2,3},{3,2},{4,5},{5,4},{6,7},{7,6},{8,9},{9,8},{10,11... | collective-permute-start | bytes 1327112 | tf_op jit(solution)/shard_map/ppermute | solution.py:51
  926.4 29.6 %collective-permute-start.73 = (bf16[864,512]{1,0:T(8,128)(2,1)}, bf16[864,512]{1,0:T(8,128)(2,1)S(1)}, u32[]{:S(2)}, u32[]{:S(2)}) collective-permute-start(bf16[864,512]{1,0:T(8,128)(2,1)} %copy-done.54), channel_id=1, source_target_pairs={{0,4},{2,6},{8,0},{10,2},{16,8},{18,10},{24,16},{26,18},{28,24},{3... | collective-permute-start | bytes 2654216 | tf_op jit(solution)/shard_map/ppermute | solution.py:92
  927.9 29.2 %collective-permute-start.70 = (bf16[864,512]{1,0:T(8,128)(2,1)}, bf16[864,512]{1,0:T(8,128)(2,1)S(1)}, u32[]{:S(2)}, u32[]{:S(2)}) collective-permute-start(bf16[864,512]{1,0:T(8,128)(2,1)} %collective-permute-done.69), channel_id=1, source_target_pairs={{0,8},{2,10},{8,16},{10,18},{16,24},{18,26},{24,28},{26,30},{28,20... | collective-permute-start | bytes 2654216 | tf_op jit(solution)/shard_map/ppermute | solution.py:92
  953.2 22.6 %collective-permute-start.96 = (bf16[864,512]{1,0:T(8,128)(2,1)S(1)}, bf16[864,512]{1,0:T(8,128)(2,1)S(1)}, u32[]{:S(2)}, u32[]{:S(2)}) collective-permute-start(bf16[864,512]{1,0:T(8,128)(2,1)S(1)} %pad_maximum_fusion.15), channel_id=1, source_target_pairs={{0,4},{2,6},{8,0},{10,2},{16,8},{18,10},{24,16},{26,18},{28,24},{3... | collective-permute-start | bytes 2654216 | tf_op jit(solution)/shard_map/ppermute | solution.py:92
  954.3 22.6 %collective-permute-start.92 = (bf16[864,512]{1,0:T(8,128)(2,1)S(1)}, bf16[864,512]{1,0:T(8,128)(2,1)}, u32[]{:S(2)}, u32[]{:S(2)}) collective-permute-start(bf16[864,512]{1,0:T(8,128)(2,1)S(1)} %pad_maximum_fusion.15), channel_id=1, source_target_pairs={{0,8},{2,10},{8,16},{10,18},{16,24},{18,26},{24,28},{26,30},{28,20... | collective-permute-start | bytes 2654216 | tf_op jit(solution)/shard_map/ppermute | solution.py:92
  956.0 38.8 %collective-permute-start.74 = (bf16[864,512]{1,0:T(8,128)(2,1)S(1)}, bf16[864,512]{1,0:T(8,128)(2,1)S(1)}, u32[]{:S(2)}, u32[]{:S(2)}) collective-permute-start(bf16[864,512]{1,0:T(8,128)(2,1)S(1)} %collective-permute-done.73), channel_id=1, source_target_pairs={{0,4},{2,6},{8,0},{10,2},{16,8},{18,10},{24,16},{26,18},{28,24},{3... | collective-permute-start | bytes 2654216 | tf_op jit(solution)/shard_map/ppermute | solution.py:92
  975.8 40.6 %collective-permute-start.97 = (bf16[864,512]{1,0:T(8,128)(2,1)S(1)}, bf16[864,512]{1,0:T(8,128)(2,1)S(1)}, u32[]{:S(2)}, u32[]{:S(2)}) collective-permute-start(bf16[864,512]{1,0:T(8,128)(2,1)S(1)} %collective-permute-done.96), channel_id=1, source_target_pairs={{0,4},{2,6},{8,0},{10,2},{16,8},{18,10},{24,16},{26,18},{28,24},{3... | collective-permute-start | bytes 2654216 | tf_op jit(solution)/shard_map/ppermute | solution.py:92
  976.9 64.6 %collective-permute-start.93 = (bf16[864,512]{1,0:T(8,128)(2,1)}, bf16[864,512]{1,0:T(8,128)(2,1)}, u32[]{:S(2)}, u32[]{:S(2)}) collective-permute-start(bf16[864,512]{1,0:T(8,128)(2,1)} %collective-permute-done.92), channel_id=1, source_target_pairs={{0,8},{2,10},{8,16},{10,18},{16,24},{18,26},{24,28},{26,30},{28,20... | collective-permute-start | bytes 2654216 | tf_op jit(solution)/shard_map/ppermute | solution.py:92
  979.0 75.3 %collective-permute-start.66 = (bf16[2,864,256]{2,1,0:T(8,128)(2,1)}, bf16[2,864,256]{2,1,0:T(8,128)(2,1)}, u32[]{:S(2)}, u32[]{:S(2)}) collective-permute-start(bf16[2,864,256]{2,1,0:T(8,128)(2,1)} %pad_maximum_fusion.12), channel_id=1, source_target_pairs={{0,1},{1,0},{2,3},{3,2},{4,5},{5,4},{6,7},{7,6},{8,9},{9,8},{10,11... | collective-permute-start | bytes 2654216 | tf_op jit(solution)/shard_map/ppermute | solution.py:379
  1015.8 51.3 %collective-permute-start.75 = (f32[2,864,256]{2,1,0:T(8,128)}, f32[2,864,256]{2,1,0:T(8,128)}, u32[]{:S(2)}, u32[]{:S(2)}) collective-permute-start(f32[2,864,256]{2,1,0:T(8,128)} %broadcast_select_fusion.7), channel_id=1, source_target_pairs={{0,1},{1,0},{2,3},{3,2},{4,5},{5,4},{6,7},{7,6},{8,9},{9,8},{10,11... | collective-permute-start | bytes 5308424 | tf_op jit(solution)/shard_map/ppermute | solution.py:59
  1040.4 59.2 %collective-permute-start.98 = (bf16[864,512]{1,0:T(8,128)(2,1)}, bf16[864,512]{1,0:T(8,128)(2,1)}, u32[]{:S(2)}, u32[]{:S(2)}) collective-permute-start(bf16[864,512]{1,0:T(8,128)(2,1)} %copy-done.50), channel_id=1, source_target_pairs={{0,4},{2,6},{8,0},{10,2},{16,8},{18,10},{24,16},{26,18},{28,24},{3... | collective-permute-start | bytes 2654216 | tf_op jit(solution)/shard_map/ppermute | solution.py:92
  1041.5 25.1 %collective-permute-start.94 = (bf16[864,512]{1,0:T(8,128)(2,1)}, bf16[864,512]{1,0:T(8,128)(2,1)}, u32[]{:S(2)}, u32[]{:S(2)}) collective-permute-start(bf16[864,512]{1,0:T(8,128)(2,1)} %collective-permute-done.93), channel_id=1, source_target_pairs={{0,8},{2,10},{8,16},{10,18},{16,24},{18,26},{24,28},{26,30},{28,20... | collective-permute-start | bytes 2654216 | tf_op jit(solution)/shard_map/ppermute | solution.py:92
  1053.9 29.5 %collective-permute-start.103 = (bf16[864,512]{1,0:T(8,128)(2,1)}, bf16[864,512]{1,0:T(8,128)(2,1)}, u32[]{:S(2)}, u32[]{:S(2)}) collective-permute-start(bf16[864,512]{1,0:T(8,128)(2,1)} %pad_maximum_fusion.17), channel_id=1, source_target_pairs={{0,8},{2,10},{8,16},{10,18},{16,24},{18,26},{24,28},{26,30},{28,20... | collective-permute-start | bytes 2654216 | tf_op jit(solution)/shard_map/ppermute | solution.py:92
  1054.3 30.0 %collective-permute-start.106 = (bf16[864,512]{1,0:T(8,128)(2,1)}, bf16[864,512]{1,0:T(8,128)(2,1)}, u32[]{:S(2)}, u32[]{:S(2)}) collective-permute-start(bf16[864,512]{1,0:T(8,128)(2,1)} %pad_maximum_fusion.17), channel_id=1, source_target_pairs={{0,4},{2,6},{8,0},{10,2},{16,8},{18,10},{24,16},{26,18},{28,24},{3... | collective-permute-start | bytes 2654216 | tf_op jit(solution)/shard_map/ppermute | solution.py:92
  1066.6 32.8 %collective-permute-start.95 = (bf16[864,512]{1,0:T(8,128)(2,1)}, bf16[864,512]{1,0:T(8,128)(2,1)S(1)}, u32[]{:S(2)}, u32[]{:S(2)}) collective-permute-start(bf16[864,512]{1,0:T(8,128)(2,1)} %collective-permute-done.94), channel_id=1, source_target_pairs={{0,8},{2,10},{8,16},{10,18},{16,24},{18,26},{24,28},{26,30},{28,20... | collective-permute-start | bytes 2654216 | tf_op jit(solution)/shard_map/ppermute | solution.py:92
  1083.4 36.6 %collective-permute-start.104 = (bf16[864,512]{1,0:T(8,128)(2,1)}, bf16[864,512]{1,0:T(8,128)(2,1)}, u32[]{:S(2)}, u32[]{:S(2)}) collective-permute-start(bf16[864,512]{1,0:T(8,128)(2,1)} %collective-permute-done.103), channel_id=1, source_target_pairs={{0,8},{2,10},{8,16},{10,18},{16,24},{18,26},{24,28},{26,30},{28,20... | collective-permute-start | bytes 2654216 | tf_op jit(solution)/shard_map/ppermute | solution.py:92
  1084.3 35.9 %collective-permute-start.107 = (bf16[864,512]{1,0:T(8,128)(2,1)}, bf16[864,512]{1,0:T(8,128)(2,1)}, u32[]{:S(2)}, u32[]{:S(2)}) collective-permute-start(bf16[864,512]{1,0:T(8,128)(2,1)} %collective-permute-done.106), channel_id=1, source_target_pairs={{0,4},{2,6},{8,0},{10,2},{16,8},{18,10},{24,16},{26,18},{28,24},{3... | collective-permute-start | bytes 2654216 | tf_op jit(solution)/shard_map/ppermute | solution.py:92
  1087.9 35.4 %collective-permute-start.77 = (bf16[2,864,256]{2,1,0:T(8,128)(2,1)}, bf16[2,864,256]{2,1,0:T(8,128)(2,1)}, u32[]{:S(2)}, u32[]{:S(2)}) collective-permute-start(bf16[2,864,256]{2,1,0:T(8,128)(2,1)} %pad_maximum_fusion.14), channel_id=1, source_target_pairs={{0,1},{1,0},{2,3},{3,2},{4,5},{5,4},{6,7},{7,6},{8,9},{9,8},{10,11... | collective-permute-start | bytes 2654216 | tf_op jit(solution)/shard_map/ppermute | solution.py:379
  1119.9 48.4 %collective-permute-start.99 = (f32[2,864,256]{2,1,0:T(8,128)}, f32[2,864,256]{2,1,0:T(8,128)S(1)}, u32[]{:S(2)}, u32[]{:S(2)}) collective-permute-start(f32[2,864,256]{2,1,0:T(8,128)} %broadcast_select_fusion.6), channel_id=1, source_target_pairs={{0,1},{1,0},{2,3},{3,2},{4,5},{5,4},{6,7},{7,6},{8,9},{9,8},{10,11... | collective-permute-start | bytes 5308424 | tf_op jit(solution)/shard_map/ppermute | solution.py:59
  1165.3 22.6 %collective-permute-start.110 = (f32[2,864,256]{2,1,0:T(8,128)S(1)}, f32[2,864,256]{2,1,0:T(8,128)S(1)}, u32[]{:S(2)}, u32[]{:S(2)}) collective-permute-start(f32[2,864,256]{2,1,0:T(8,128)S(1)} %broadcast_select_fusion.5), channel_id=1, source_target_pairs={{0,1},{1,0},{2,3},{3,2},{4,5},{5,4},{6,7},{7,6},{8,9},{9,8},{10,11... | collective-permute-start | bytes 5308424 | tf_op jit(solution)/shard_map/ppermute | solution.py:59
  1188.7 22.6 %collective-permute-start.101 = (bf16[2,864,256]{2,1,0:T(8,128)(2,1)S(1)}, bf16[2,864,256]{2,1,0:T(8,128)(2,1)S(1)}, u32[]{:S(2)}, u32[]{:S(2)}) collective-permute-start(bf16[2,864,256]{2,1,0:T(8,128)(2,1)S(1)} %pad_maximum_fusion.16), channel_id=1, source_target_pairs={{0,1},{1,0},{2,3},{3,2},{4,5},{5,4},{6,7},{7,6},{8,9},{9,8},{10,11... | collective-permute-start | bytes 2654216 | tf_op jit(solution)/shard_map/ppermute | solution.py:379
  1191.8 38.2 %collective-permute-start.112 = (bf16[2,864,256]{2,1,0:T(8,128)(2,1)S(1)}, bf16[2,864,256]{2,1,0:T(8,128)(2,1)S(1)}, u32[]{:S(2)}, u32[]{:S(2)}) collective-permute-start(bf16[2,864,256]{2,1,0:T(8,128)(2,1)S(1)} %pad_maximum_fusion.18), channel_id=1, source_target_pairs={{0,1},{1,0},{2,3},{3,2},{4,5},{5,4},{6,7},{7,6},{8,9},{9,8},{10,11... | collective-permute-start | bytes 2654216 | tf_op jit(solution)/shard_map/ppermute | solution.py:379
  (131 other events, 1525.7 us)
